TPU v7x, 512 devices: a whole 4x8x8 slice. The times are simulated.
512 devices in a mesh: dp: 8 (over x, core), ctx: 64 (over z, y).
Axes of the slice: x: 4, y: 8, z: 8, core: 2. Of those that a mesh axis runs over, the one named last changes fastest.
Arguments:
- queries: bfloat16 [8, 32768, 256], P('dp', 'ctx'), may hold values from -6 to 6
- keys: bfloat16 [8, 32768, 256], P('dp', 'ctx'), may hold values from -6 to 6
- values: bfloat16 [8, 32768, 256], P('dp', 'ctx'), may hold values from -6 to 6
- out_grad: bfloat16 [8, 32768, 256], P('dp', 'ctx'), may hold values from -6 to 6
- q_gain: float32 [256], replicated, may hold values from 0.25 to 1.75
- offsets: int32 [8, 64], P('dp', 'ctx'), may hold values from 0 to 131071
Outputs:
- grad_queries: bfloat16 [8, 32768, 256], P('dp', 'ctx')
- grad_keys: bfloat16 [8, 32768, 256], P('dp', 'ctx')
- grad_values: bfloat16 [8, 32768, 256], P('dp', 'ctx')
- grad_gain: float32 [256], replicated
All inputs are finite; a program needn't handle non-finite values.
Results may differ from a plain program's by a relative error of at most 0.011.
Values sent between devices are 32-bit elements; how exact they have to be, the bound alone decides.
No kernel may reach another device: no remote copies, remote signals or barrier semaphores. Data moves between devices by JAX's collectives and lax.ppermute only.
A program may use at most 128 MiB of HBM per device.

v0:
```python
import jax
import jax.numpy as jnp
from jax import lax
from jax.sharding import PartitionSpec as P

HEADS = 2
HEAD_DIM = 128
BLOCK = 512


def prefix(value, axis, join, neutral, backward):
    count, mine = (lax.axis_size(axis), lax.axis_index(axis))
    pieces = lax.all_gather(value, axis)
    if backward:
        pieces = pieces[::-1]
        mine = count - 1 - mine
    running = jnp.full_like(value, 0) + jnp.asarray(neutral, value.dtype)

    def hop(position, running):
        longer = join(running, pieces[position])
        return jnp.where(position < mine, longer, running)

    return lax.fori_loop(0, count - 1, hop, running)


def rotate(field, position, sign):
    half = field.shape[-1] // 2
    freqs = jnp.power(
        jnp.float32(500000.0), -(2.0 * jnp.arange(half, dtype=jnp.float32)) / field.shape[-1]
    )
    angle = position.astype(jnp.float32)[:, None] * freqs[None, :]
    cosine = jnp.cos(angle)[:, None, :]
    sine = sign * jnp.sin(angle)[:, None, :]
    first = field[..., :half]
    second = field[..., half:]
    return jnp.concatenate(
        [first * cosine - second * sine, second * cosine + first * sine], axis=-1
    )


def shard_grads(query_rot, key_rot, value_rows, grad_rows, state_in, back_in, scale):
    rows = query_rot.shape[0]
    nblocks = rows // BLOCK
    shape = (nblocks, BLOCK, HEADS, HEAD_DIM)
    qb = query_rot.reshape(shape)
    kb = key_rot.reshape(shape)
    vb = value_rows.reshape(shape)
    ob = grad_rows.reshape(shape)
    kvb = jnp.einsum("nthd,nthe->nhde", kb, vb, preferred_element_type=jnp.float32)
    qob = jnp.einsum("nthd,nthe->nhde", qb, ob, preferred_element_type=jnp.float32)
    empty = jnp.zeros((1, HEADS, HEAD_DIM, HEAD_DIM), jnp.float32)
    forward_sum = jnp.concatenate([empty, jnp.cumsum(kvb, axis=0)[:-1]], axis=0)
    backward_sum = jnp.concatenate([jnp.cumsum(qob[::-1], axis=0)[::-1][1:], empty], axis=0)
    state_low = (state_in[None] + forward_sum).astype(jnp.bfloat16)
    back_low = (back_in[None] + backward_sum).astype(jnp.bfloat16)
    causal = jnp.arange(BLOCK)[:, None] >= jnp.arange(BLOCK)[None, :]
    scores = jnp.einsum("nthd,nshd->nhts", qb, kb, preferred_element_type=jnp.float32)
    attn = jnp.where(causal[None, None], scale * scores, 0.0).astype(jnp.bfloat16)
    dscores = jnp.einsum("nthe,nshe->nhts", ob, vb, preferred_element_type=jnp.float32)
    dattn = jnp.where(causal[None, None], scale * dscores, 0.0).astype(jnp.bfloat16)
    dquery = jnp.einsum(
        "nhts,nshd->nthd", dattn, kb, preferred_element_type=jnp.float32
    ) + scale * jnp.einsum("nthe,nhde->nthd", ob, state_low, preferred_element_type=jnp.float32)
    dkey = jnp.einsum(
        "nhts,nthd->nshd", dattn, qb, preferred_element_type=jnp.float32
    ) + scale * jnp.einsum("nshe,nhde->nshd", vb, back_low, preferred_element_type=jnp.float32)
    dvalue = jnp.einsum(
        "nhts,nthe->nshe", attn, ob, preferred_element_type=jnp.float32
    ) + scale * jnp.einsum("nshd,nhde->nshe", kb, back_low, preferred_element_type=jnp.float32)
    flat = (rows, HEADS, HEAD_DIM)
    return (dquery.reshape(flat), dkey.reshape(flat), dvalue.reshape(flat))


def add_states(earlier, later):
    return earlier + later


def local(queries, keys, values, out_grad, q_gain, offsets):
    rows = queries.shape[1]
    width = queries.shape[2]
    seq_tokens = rows * lax.axis_size("ctx")
    all_tokens = seq_tokens * lax.axis_size("dp")
    scale = (HEAD_DIM * seq_tokens) ** (-0.5)
    position = offsets[0, 0] + jnp.arange(rows, dtype=jnp.int32)
    heads_shape = (rows, HEADS, HEAD_DIM)
    query_float = queries[0].astype(jnp.float32)
    query_rot = rotate((query_float * q_gain).reshape(heads_shape), position, 1.0).astype(
        jnp.bfloat16
    )
    key_rot = rotate(keys[0].astype(jnp.float32).reshape(heads_shape), position, 1.0).astype(
        jnp.bfloat16
    )
    value_rows = values[0].reshape(heads_shape)
    grad_rows = out_grad[0].reshape(heads_shape)
    kv_shard = jnp.einsum("thd,the->hde", key_rot, value_rows, preferred_element_type=jnp.float32)
    qo_shard = jnp.einsum("thd,the->hde", query_rot, grad_rows, preferred_element_type=jnp.float32)
    zeros = jnp.zeros_like(kv_shard)
    state_in = prefix(kv_shard, "ctx", add_states, zeros, False)
    back_in = prefix(qo_shard, "ctx", add_states, zeros, True)
    dquery, dkey, dvalue = shard_grads(
        query_rot, key_rot, value_rows, grad_rows, state_in, back_in, scale
    )
    dqs = rotate(dquery, position, -1.0).reshape(rows, width)
    dks = rotate(dkey, position, -1.0).reshape(rows, width)
    gain_part = jnp.sum(dqs * query_float, axis=0)
    grad_gain = lax.psum(gain_part, ("dp", "ctx")) * all_tokens ** (-0.5)
    grad_queries = (dqs * q_gain).astype(jnp.bfloat16)[None]
    grad_keys = dks.astype(jnp.bfloat16)[None]
    grad_values = dvalue.reshape(rows, width).astype(jnp.bfloat16)[None]
    return (grad_queries, grad_keys, grad_values, grad_gain)


def solution(mesh):
    in_specs = (
        P("dp", "ctx", None),
        P("dp", "ctx", None),
        P("dp", "ctx", None),
        P("dp", "ctx", None),
        P(),
        P("dp", "ctx"),
    )
    out_specs = (P("dp", "ctx", None), P("dp", "ctx", None), P("dp", "ctx", None), P())
    return jax.shard_map(local, mesh=mesh, in_specs=in_specs, out_specs=out_specs, check_vma=False)
```

profile of v0, /device:TPU:1, one launch (start us, length us, event | category | flops | bytes accessed | tf_op | source)
XLA Modules:
  0.0 387.9 jit_solution(7784871391069560485)
XLA Ops:
  7.9 1.1 copy.31
  9.0 1.1 copy.25
  10.1 1.1 copy.42
  14.7 103.2 %all-gather.7.cloned.1.call-done = f32[128,128,128]{2,1,0:T(8,128)} async-done(((f32[2,128,128]{2,1,0:T(8,128)}), f32[128,128,128]{2,1,0:T(8,128)}) %all-gather.7.cloned.1.call-update) | async-done | bytes 8388624 | tf_op jit(solution)/shard_map/all_gather | solution.py:13
  117.9 7.7 %rev.3 = f32[64,2,128,128]{3,2,1,0:T(8,128)} reverse(f32[64,2,128,128]{3,2,1,0:T(8,128)} %bitcast.47), dimensions={0} | reverse | bytes 16777216 | tf_op jit(solution)/shard_map/rev | solution.py:15
  125.7 61.4 %while.29 = (s32[]{:T(128)}, f32[2,128,128]{2,1,0:T(8,128)S(1)}, s32[]{:T(128)}, f32[64,2,128,128]{3,2,1,0:T(8,128)}, s32[]{:T(128)}, /*index=5*/s32[]{:T(128)}) while((s32[]{:T(128)}, f32[2,128,128]{2,1,0:T(8,128)S(1)}, s32[]{:T(128)}, f32[64,2,128,128]{3,2,1,0:T(8,128)}, s32[]{:T(128)}, /*index=5*/s32[]{:T(128)}) %tuple.76), condition=%wide.region_3.4_spmd.clone, body=%wide.region_2.3_spmd.clone.sunk | while | flops 98308 | bytes 393309 | solution.py:23
  126.6 0.9 add_select_fusion.5
  127.6 0.9 add_select_fusion.5
  128.6 0.9 add_select_fusion.5
  129.6 0.9 add_select_fusion.5
  130.5 0.9 add_select_fusion.5
  131.5 0.9 add_select_fusion.5
  132.5 0.9 add_select_fusion.5
  133.4 1.0 add_select_fusion.5
  134.4 1.0 add_select_fusion.5
  135.4 1.0 add_select_fusion.5
  136.4 0.9 add_select_fusion.5
  137.4 0.9 add_select_fusion.5
  138.3 0.9 add_select_fusion.5
  139.3 1.0 add_select_fusion.5
  140.3 0.9 add_select_fusion.5
  141.3 0.9 add_select_fusion.5
  142.2 0.9 add_select_fusion.5
  143.2 0.9 add_select_fusion.5
  144.2 0.9 add_select_fusion.5
  145.1 0.9 add_select_fusion.5
  146.1 0.9 add_select_fusion.5
  147.1 1.0 add_select_fusion.5
  148.1 0.9 add_select_fusion.5
  149.0 0.9 add_select_fusion.5
  150.0 0.9 add_select_fusion.5
  151.0 0.9 add_select_fusion.5
  152.0 0.9 add_select_fusion.5
  152.9 0.9 add_select_fusion.5
  153.9 0.9 add_select_fusion.5
  154.9 0.9 add_select_fusion.5
  155.9 0.9 add_select_fusion.5
  156.8 0.9 add_select_fusion.5
  174.3 1.0 add_select_fusion.5
  181.2 1.0 add_select_fusion.5
  182.2 1.0 add_select_fusion.5
  184.2 1.0 add_select_fusion.5
  185.1 1.0 add_select_fusion.5
  187.4 1.4 fusion.5
  188.8 1.8 copy.39
  190.8 28.3 %all-gather.5.cloned.1.call-done = f32[128,128,128]{2,1,0:T(8,128)} async-done(((f32[2,128,128]{2,1,0:T(8,128)}), f32[128,128,128]{2,1,0:T(8,128)}) %all-gather.5.cloned.1.call-update) | async-done | bytes 8388624 | tf_op jit(solution)/shard_map/all_gather | solution.py:13
  219.1 61.3 %while.28 = (s32[]{:T(128)}, f32[2,128,128]{2,1,0:T(8,128)S(1)}, s32[]{:T(128)}, f32[64,2,128,128]{3,2,1,0:T(8,128)}, s32[]{:T(128)}, /*index=5*/s32[]{:T(128)}) while((s32[]{:T(128)}, f32[2,128,128]{2,1,0:T(8,128)S(1)}, s32[]{:T(128)}, f32[64,2,128,128]{3,2,1,0:T(8,128)}, s32[]{:T(128)}, /*index=5*/s32[]{:T(128)}) %tuple.86), condition=%wide.region_1.2_spmd.clone, body=%wide.region_0.1_spmd.clone.sunk | while | flops 98308 | bytes 393309 | solution.py:23
  283.5 97.0 %psum.7 = f32[256]{0:T(256)S(1)} all-reduce(f32[256]{0:T(256)S(1)} %get-tuple-element.226), channel_id=1, replica_groups=mesh['dp'=8,'ctx'=64] {'dp','ctx'}, use_global_device_ids=true, to_apply=%region_5.6 | all-reduce | flops 256 | bytes 2048 | tf_op jit(solution)/shard_map/psum | solution.py:106
  (123 shorter events, 92.1 us)
Async XLA Ops:
  7.2 4.6 %copy-start.2 = (f32[256]{0:T(256)S(1)}, f32[256]{0:T(256)}, u32[]{:S(2)}) copy-start(f32[256]{0:T(256)} %param.14) | copy-start | bytes 3076
  7.2 110.8 %all-gather.7.cloned.1.call-start = ((), (), s32[]{:S(2)}) async-start(), calls=%async_computation.1 | async-start | bytes 8519680 | tf_op jit(solution)/shard_map/all_gather | solution.py:13
  11.2 1.8 copy-start.1
  13.0 206.1 %all-gather.5.cloned.1.call-start = ((), (), s32[]{:S(2)}) async-start(), calls=%async_computation | async-start | bytes 8519680 | tf_op jit(solution)/shard_map/all_gather | solution.py:13
  281.6 1.1 copy-start
Sparse Core Ops, SparseCore 0:
  13.1 104.8 all-gather.6
  121.6 97.4 all-gather.4
where the time goes:
time: 390 us; the launch traced here: 388 us
  waiting for transfers between devices  132 us (34%)
  other arithmetic  122 us (31%)
  blocking collectives  97 us (25%)
  between operations  14.9 us (4%)
  local copies, waits for them, and re-layouts  13.9 us (4%)
  matrix products  5.26 us (1%)
    all_gather x2, waiting for transfers between devices, prefix(): pieces = lax.all_gather(value, axis)  131 us
    select_n x126, other arithmetic, hop(): return jnp.where(position < mine, longer, running)  120 us
    psum x1, blocking collectives, local(): grad_gain = lax.psum(gain_part, ('dp', 'ctx')) * all_tokens ** (-0.5)  97 us
  transfers between devices with their start and end apart: 2, of which 2 were waited for; matrix products, arithmetic and copies ran while one was open for 19% of the time, Pallas kernels for 0%

commit v1 on v0

v1 whole, which is shorter than its diff:
```python
import functools

import jax
import jax.numpy as jnp
import numpy as np
from jax import lax
from jax.experimental import pallas as pl
from jax.experimental.pallas import tpu as pltpu
from jax.sharding import PartitionSpec as P

HEADS = 2
DIM = 128
HALF = 64
ROWS = 512
BASE = 500000.0
LOW, MIDDLE, HIGH = 32, 64, 65
TABLE = HIGH + MIDDLE + LOW
TABLE_ROWS = 168
PIECE = 16


def rotary_tables():
    freqs = np.power(BASE, -2.0 * np.arange(HALF) / DIM).astype(np.float32).astype(np.float64)
    steps = np.concatenate([np.arange(HIGH) * 2048, np.arange(MIDDLE) * 32, np.arange(LOW)])
    angle = np.zeros((TABLE_ROWS, HALF))
    angle[:TABLE] = steps[:, None] * freqs[None, :]
    cosine, sine = np.cos(angle), np.sin(angle)
    return (
        np.concatenate([cosine, cosine], axis=1).astype(np.float32),
        np.concatenate([-sine, sine], axis=1).astype(np.float32),
    )


def dot(a, b, ca, cb):
    return lax.dot_general(a, b, (((ca,), (cb,)), ((), ())), preferred_element_type=jnp.float32)


def swap(x):
    return pltpu.roll(x, HALF, 1)


def states_kernel(off_ref, ctab_ref, stab_ref, q_ref, k_ref, v_ref, g_ref, send_ref, krot_ref, cos_ref, sin_ref):
    offset = off_ref[0, 0]
    high, middle, low = offset // 2048, (offset // 32) % 64, offset % 32

    def row(at):
        return ctab_ref[pl.ds(at, 1), :], stab_ref[pl.ds(at, 1), :]

    def add(left, right):
        (ca, sa), (cb, sb) = left, right
        return ca * cb - sa * sb, sa * cb + ca * sb

    start = add(add(row(high), row(HIGH + middle)), row(HIGH + MIDDLE + low))
    lows = (
        ctab_ref[HIGH + MIDDLE : HIGH + MIDDLE + LOW, :],
        stab_ref[HIGH + MIDDLE : HIGH + MIDDLE + LOW, :],
    )
    for block in range(ROWS // LOW):
        here = add(start, row(HIGH + block))
        cosine, sine = add(here, lows)
        cos_ref[block * LOW : (block + 1) * LOW, :] = cosine
        sin_ref[block * LOW : (block + 1) * LOW, :] = sine
    cosine, sine = cos_ref[...], sin_ref[...]
    for head in range(HEADS):
        lanes = slice(head * DIM, (head + 1) * DIM)
        q = q_ref[0, :, lanes].astype(jnp.float32)
        k = k_ref[0, :, lanes].astype(jnp.float32)
        krot = (k * cosine + swap(k) * sine).astype(jnp.bfloat16)
        krot_ref[:, lanes] = krot
        kv = dot(krot, v_ref[0, :, lanes], 0, 0)
        g = g_ref[0, :, lanes]
        qcos = dot((q * cosine).astype(jnp.bfloat16), g, 0, 0)
        qsin = dot((q * -sine).astype(jnp.bfloat16), g, 0, 0)
        for half in range(2):
            at = 2 * head + half
            rows = slice(half * HALF, (half + 1) * HALF)
            other = slice((1 - half) * HALF, (2 - half) * HALF)
            send_ref[:, at, :] = kv[rows]
            send_ref[:, 4 + at, :] = kv[rows]
            send_ref[:, 8 + at, :] = qcos[rows]
            send_ref[:, 12 + at, :] = qsin[other]


def local_kernel(
    scale, gain_ref, cos_ref, sin_ref, q_ref, krot_ref, v_ref, g_ref, dq_ref, dk_ref, dv_ref, part_ref
):
    cosine, sine = cos_ref[...], sin_ref[...]
    causal = lax.broadcasted_iota(jnp.int32, (ROWS, ROWS), 0) >= lax.broadcasted_iota(
        jnp.int32, (ROWS, ROWS), 1
    )
    part_ref[...] = jnp.zeros_like(part_ref)
    for head in range(HEADS):
        lanes = slice(head * DIM, (head + 1) * DIM)
        q = q_ref[0, :, lanes].astype(jnp.float32)
        scaled = q * gain_ref[:, lanes]
        qrot = (scaled * cosine + swap(scaled) * sine).astype(jnp.bfloat16)
        krot = krot_ref[:, lanes]
        v = v_ref[0, :, lanes]
        g = g_ref[0, :, lanes]
        attn = jnp.where(causal, scale * dot(qrot, krot, 1, 1), 0.0).astype(jnp.bfloat16)
        dattn = jnp.where(causal, scale * dot(g, v, 1, 1), 0.0).astype(jnp.bfloat16)
        dv_ref[:, lanes] = dot(attn, g, 0, 0)
        dk = dot(dattn, qrot, 0, 0)
        dk_ref[:, lanes] = dk * cosine - swap(dk) * sine
        dq = dot(dattn, krot, 1, 0)
        dq = dq * cosine - swap(dq) * sine
        dq_ref[:, lanes] = dq
        part_ref[head : head + 1, :] = jnp.sum(dq * q, axis=0, keepdims=True)


def scan_kernel(scale, axis, gain_ref, recv_ref, part_ref, send_ref):
    count = recv_ref.shape[0]
    mine = lax.axis_index(axis)
    rows = lax.broadcasted_iota(jnp.int32, (8, DIM), 0)
    gains = [gain_ref[half * HALF + mine] for half in range(4)]
    weight = jnp.zeros((8, DIM), jnp.float32)
    for at, source in enumerate((0, 1, 2, 3, 1, 0, 3, 2)):
        weight = jnp.where(rows == at, gains[source], weight)

    before = jnp.zeros((8, DIM), jnp.float32)
    products = jnp.zeros((8, DIM), jnp.float32)
    for shard in range(count):
        send_ref[shard, 0:8, :] = before
        products += before * recv_ref[shard, 8:16, :]
        before += recv_ref[shard, 0:8, :]
    after = jnp.zeros((8, DIM), jnp.float32)
    for shard in reversed(range(count)):
        back = after * weight
        back = back + pltpu.roll(back, 4, 0)
        send_ref[shard, 0:8, :] = jnp.where(rows < 4, send_ref[shard, 0:8, :], back)
        after += recv_ref[shard, 8:16, :]

    sums = scale * jnp.sum(products, axis=1, keepdims=True)
    lane = lax.broadcasted_iota(jnp.int32, (8, DIM), 1)
    part = part_ref[...]
    for head in range(HEADS):
        for half in range(2):
            at = 2 * head + half
            other = 4 + 2 * head + 1 - half
            value = sums[at : at + 1] + sums[other : other + 1]
            hit = (rows == head) & (lane == mine + half * HALF)
            part = part + jnp.where(hit, value, 0.0)
    for shard in range(count):
        send_ref[shard, 8:16, :] = part


def gain_kernel(recv_ref, out_ref):
    out_ref[...] = jnp.sum(recv_ref[:, 8:16, :], axis=0)


def final_kernel(
    scale, gain_ref, cos_ref, sin_ref, krot_ref, v_ref, g_ref, dq_ref, dk_ref, dv_ref, recv_ref,
    gq_ref, gk_ref, gv_ref,
):
    cosine, sine = cos_ref[...], sin_ref[...]
    for head in range(HEADS):
        lanes = slice(head * DIM, (head + 1) * DIM)

        def matrix(first):
            return jnp.concatenate(
                [recv_ref[:, first, :], recv_ref[:, first + 1, :]], axis=0
            ).astype(jnp.bfloat16)

        state = matrix(2 * head)
        back = matrix(4 + 2 * head)
        dq = scale * dot(g_ref[0, :, lanes], state, 1, 1)
        dq = dq_ref[:, lanes] + (dq * cosine - swap(dq) * sine)
        gq_ref[0, :, lanes] = (dq * gain_ref[:, lanes]).astype(jnp.bfloat16)
        dk = scale * dot(v_ref[0, :, lanes], back, 1, 1)
        gk_ref[0, :, lanes] = (dk_ref[:, lanes] + (dk * cosine - swap(dk) * sine)).astype(jnp.bfloat16)
        dv = scale * dot(krot_ref[:, lanes], back, 1, 0)
        gv_ref[0, :, lanes] = (dv_ref[:, lanes] + dv).astype(jnp.bfloat16)


def total_kernel(factor, parts_ref, out_ref):
    out_ref[...] = jnp.sum(parts_ref[...], axis=0) * factor


VMEM = pl.BlockSpec(memory_space=pltpu.VMEM)
SMEM = pl.BlockSpec(memory_space=pltpu.SMEM)
PARAMS = pltpu.CompilerParams(vmem_limit_bytes=40 * 1024 * 1024)


def shape(*dims, dtype=jnp.float32):
    return jax.ShapeDtypeStruct(dims, dtype)


def local(queries, keys, values, out_grad, q_gain, offsets):
    rows, width = queries.shape[1], queries.shape[2]
    shards = lax.axis_size("ctx")
    all_tokens = rows * shards * lax.axis_size("dp")
    scale = float((DIM * rows * shards) ** (-0.5))
    cos_table, sin_table = rotary_tables()
    gain_row = q_gain.reshape(1, width)

    sent, krot, cosine, sine = pl.pallas_call(
        states_kernel,
        out_shape=(
            shape(shards, PIECE, DIM),
            shape(rows, width, dtype=jnp.bfloat16),
            shape(rows, DIM),
            shape(rows, DIM),
        ),
        in_specs=[SMEM] + [VMEM] * 6,
        out_specs=(VMEM,) * 4,
        compiler_params=PARAMS,
        name="states",
    )(offsets, jnp.asarray(cos_table), jnp.asarray(sin_table), queries, keys, values, out_grad)

    received = lax.all_to_all(sent, "ctx", 0, 0, tiled=True)

    dq, dk, dv, part = pl.pallas_call(
        functools.partial(local_kernel, scale),
        out_shape=(shape(rows, width), shape(rows, width), shape(rows, width), shape(8, DIM)),
        in_specs=[VMEM] * 7,
        out_specs=(VMEM,) * 4,
        compiler_params=PARAMS,
        name="local_grads",
    )(gain_row, cosine, sine, queries, krot, values, out_grad)

    scanned = pl.pallas_call(
        functools.partial(scan_kernel, scale, "ctx"),
        out_shape=shape(shards, PIECE, DIM),
        in_specs=[SMEM, VMEM, VMEM],
        out_specs=VMEM,
        compiler_params=PARAMS,
        name="scan",
    )(q_gain, received, part)

    states = lax.all_to_all(scanned, "ctx", 0, 0, tiled=True)

    gain_part = pl.pallas_call(
        gain_kernel,
        out_shape=shape(8, DIM),
        in_specs=[VMEM],
        out_specs=VMEM,
        compiler_params=PARAMS,
        name="gain_part",
    )(states)
    gathered = lax.all_gather(gain_part, "dp")

    grad_queries, grad_keys, grad_values = pl.pallas_call(
        functools.partial(final_kernel, scale),
        out_shape=(shape(1, rows, width, dtype=jnp.bfloat16),) * 3,
        in_specs=[VMEM] * 10,
        out_specs=(VMEM,) * 3,
        compiler_params=PARAMS,
        name="final",
    )(gain_row, cosine, sine, krot, values, out_grad, dq, dk, dv, states)

    total = pl.pallas_call(
        functools.partial(total_kernel, float(all_tokens ** (-0.5))),
        out_shape=shape(8, DIM),
        in_specs=[VMEM],
        out_specs=VMEM,
        name="gain_total",
    )(gathered)
    grad_gain = total[:HEADS].reshape(width)
    return grad_queries, grad_keys, grad_values, grad_gain


def solution(mesh):
    rows = P("dp", "ctx", None)
    return jax.shard_map(
        local,
        mesh=mesh,
        in_specs=(rows, rows, rows, rows, P(), P("dp", "ctx")),
        out_specs=(rows, rows, rows, P()),
        check_vma=False,
    )
```

time: 390 us -> 90.2 us (0.23)
  other arithmetic: 122 us -> 0 us
  waiting for transfers between devices: 132 us -> 13.9 us
  blocking collectives: 97 us -> 40.8 us
  starting transfers between devices: 0.08 us -> 17.3 us
  between operations: 14.9 us -> 1.36 us
  Pallas kernels: 0 us -> 7.01 us
  matrix products: 5.26 us -> 0 us
  local copies, waits for them, and re-layouts: 13.9 us -> 9.3 us
    all_gather x2 -> x0, waiting for transfers between devices: 131 us -> none  [prefix(): pieces = lax.all_gather(value, axis)]
    select_n x126 -> x0, other arithmetic: 120 us -> none  [hop(): return jnp.where(position < mine, longer, running)]
    psum x1 -> x0, blocking collectives: 97 us -> none  [local(): grad_gain = lax.psum(gain_part, ('dp', 'ctx')) * all_tokens ** (-0.5)]
    all_to_all x0 -> x1, blocking collectives: none -> 22.4 us  [local(): states = lax.all_to_all(scanned, 'ctx', 0, 0, tiled=True)]
    all_gather x0 -> x1, blocking collectives: none -> 18.4 us  [local(): gathered = lax.all_gather(gain_part, 'dp')]
    all_to_all x0 -> x1, starting transfers between devices: none -> 17.3 us  [local(): received = lax.all_to_all(sent, 'ctx', 0, 0, tiled=True)]
    all_to_all x0 -> x1, waiting for transfers between devices: none -> 13.9 us  [local(): received = lax.all_to_all(sent, 'ctx', 0, 0, tiled=True)]
    rev x1 -> x0, local copies, waits for them, and re-layouts: 7.72 us -> none  [prefix(): pieces = pieces[::-1]]
  transfers between devices with their start and end apart: 2 -> 1, of which waited for: 2 -> 1; matrix products, arithmetic and copies ran while one was open for 19% -> 0% of each run, Pallas kernels for 0% -> 2%
where the time goes in v1:
time: 90.2 us; the launch traced here: 89.6 us
  blocking collectives  40.8 us (45%)
  starting transfers between devices  17.3 us (19%)
  waiting for transfers between devices  13.9 us (15%)
  local copies, waits for them, and re-layouts  9.3 us (10%)
  Pallas kernels  7.01 us (8%)
  between operations  1.36 us (2%)
    all_to_all x1, blocking collectives, local(): states = lax.all_to_all(scanned, 'ctx', 0, 0, tiled=True)  22.4 us
    all_gather x1, blocking collectives, local(): gathered = lax.all_gather(gain_part, 'dp')  18.4 us
    all_to_all x1, starting transfers between devices, local(): received = lax.all_to_all(sent, 'ctx', 0, 0, tiled=True)  17.3 us
    all_to_all x1, waiting for transfers between devices, local(): received = lax.all_to_all(sent, 'ctx', 0, 0, tiled=True)  13.9 us
    unnamed x24, local copies, waits for them, and re-layouts  8.05 us
  transfers between devices with their start and end apart: 1, of which 1 were waited for; matrix products, arithmetic and copies ran while one was open for 0% of the time, Pallas kernels for 2%

profile of v1, /device:TPU:1, one launch (start us, length us, event | category | flops | bytes accessed | tf_op | source)
XLA Modules:
  0.0 89.6 jit_solution(14763233534467326695)
XLA Ops:
  1.3 0.0 copy-start
  1.3 0.9 %copy-done = bf16[1,512,256]{2,1,0:T(8,128)(2,1)S(1)} copy-done((bf16[1,512,256]{2,1,0:T(8,128)(2,1)S(1)}, bf16[1,512,256]{2,1,0:T(8,128)(2,1)}, u32[]{:S(2)}) %copy-start) | copy-done | bytes 262168
  2.2 0.0 copy-start.2
  2.2 0.9 %copy-done.2 = bf16[1,512,256]{2,1,0:T(8,128)(2,1)S(1)} copy-done((bf16[1,512,256]{2,1,0:T(8,128)(2,1)S(1)}, bf16[1,512,256]{2,1,0:T(8,128)(2,1)}, u32[]{:S(2)}) %copy-start.2) | copy-done | bytes 262168
  3.2 0.0 copy-start.4
  3.2 0.9 %copy-done.4 = bf16[1,512,256]{2,1,0:T(8,128)(2,1)S(1)} copy-done((bf16[1,512,256]{2,1,0:T(8,128)(2,1)S(1)}, bf16[1,512,256]{2,1,0:T(8,128)(2,1)}, u32[]{:S(2)}) %copy-start.4) | copy-done | bytes 262168
  4.1 0.0 copy-start.8
  4.1 0.9 %copy-done.8 = bf16[1,512,256]{2,1,0:T(8,128)(2,1)S(1)} copy-done((bf16[1,512,256]{2,1,0:T(8,128)(2,1)S(1)}, bf16[1,512,256]{2,1,0:T(8,128)(2,1)}, u32[]{:S(2)}) %copy-start.8) | copy-done | bytes 262168
  5.1 0.0 copy-start.9
  5.1 0.9 copy-done.9
  6.0 0.0 copy-start.10
  6.0 0.9 copy-done.10
  6.9 1.6 %states.1 = (f32[64,16,128]{2,1,0:T(8,128)}, bf16[512,256]{1,0:T(8,128)(2,1)S(1)}, f32[512,128]{1,0:T(8,128)S(1)}, f32[512,128]{1,0:T(8,128)S(1)}) custom-call(s32[1,1]{1,0:T(1,128)S(6)} %copy.12.off_ref, f32[168,128]{1,0:T(8,128)S(1)} %copy-done.10, f32[168,128]{1,0:T(8,128)S(1)} %copy-done.9, bf16[1,512,256]{2,1,0:T(8,128)(2,1)S(1)} %copy-done.4, ...), custom_call_target="tpu_custom_call" | custom-call | tf_op jit(solution)/shard_map/states/pallas_call | solution.py:196
  8.4 0.0 copy-start.1
  8.4 0.0 copy-start.3
  8.4 0.0 copy-start.5
  8.4 17.3 %all-to-all-start = ((f32[64,16,128]{2,1,0:T(8,128)}), f32[64,16,128]{2,1,0:T(8,128)S(1)}, u32[]{:S(2)}, u32[]{:S(2)}) async-start(f32[64,16,128]{2,1,0:T(8,128)} %get-tuple-element.21), calls=%async_computation | async-start | bytes 1048576 | tf_op jit(solution)/shard_map/all_to_all | solution.py:210
  25.7 0.0 copy-start.11
  25.7 0.0 copy-done.1
  25.7 0.0 copy-done.3
  25.8 0.0 copy-done.5
  25.8 0.6 copy-done.11
  26.4 1.8 %local_grads.1 = (f32[512,256]{1,0:T(8,128)S(1)}, f32[512,256]{1,0:T(8,128)S(1)}, f32[512,256]{1,0:T(8,128)S(1)}, f32[8,128]{1,0:T(8,128)S(1)}) custom-call(f32[1,256]{1,0:T(1,128)S(1)} %bitcast.4, f32[512,128]{1,0:T(8,128)S(1)} %get-tuple-element.15.cos_ref, f32[512,128]{1,0:T(8,128)S(1)} %get-tuple-element.16.sin_ref, bf16[1,512,256]{2,1,0:T(8,128)(2,1)S(1)} %copy-done.5, ...), custom_call_target="tpu_custom_call" | custom-call | tf_op jit(solution)/shard_map/local_grads/pallas_call | solution.py:212
  28.2 0.0 copy-start.6
  28.2 0.8 copy-done.6
  29.0 13.9 %all-to-all-done.recv_ref = f32[64,16,128]{2,1,0:T(8,128)S(1)} async-done(((f32[64,16,128]{2,1,0:T(8,128)}), f32[64,16,128]{2,1,0:T(8,128)S(1)}, u32[]{:S(2)}, u32[]{:S(2)}) %all-to-all-start) | async-done | bytes 524320 | tf_op jit(solution)/shard_map/all_to_all | solution.py:210
  42.9 0.8 scan.1
  43.7 22.4 %all_to_all.10.recv_ref = f32[64,16,128]{2,1,0:T(8,128)S(1)} all-to-all(f32[64,16,128]{2,1,0:T(8,128)S(1)} %scan.1), channel_id=1, replica_groups=mesh['dp'=8,'ctx'=64] {'ctx'}, dimensions={0} | all-to-all | bytes 1048576 | tf_op jit(solution)/shard_map/all_to_all | solution.py:230
  66.1 0.1 gain_part.1
  66.2 18.4 %all-gather = f32[64,128]{1,0:T(8,128)} all-gather(f32[8,128]{1,0:T(8,128)S(1)} %gain_part.1), channel_id=2, replica_groups=mesh['dp'=8,'ctx'=64] {'dp'}, dimensions={0}, use_global_device_ids=true | all-gather | bytes 36864 | tf_op jit(solution)/shard_map/all_gather | solution.py:240
  84.5 1.4 %gain_total.1 = f32[8,128]{1,0:T(8,128)} custom-call(f32[8,8,128]{2,1,0:T(8,128)} %bitcast.6), custom_call_target="tpu_custom_call" | custom-call | tf_op jit(solution)/shard_map/gain_total/pallas_call | solution.py:251
  85.9 1.2 %slice_bitcast_fusion = f32[256]{0:T(256)} fusion(f32[8,128]{1,0:T(8,128)} %gain_total.1), kind=kLoop, calls=%fused_computation | loop fusion | bytes 2048 | tf_op jit(solution)/shard_map/reshape | solution.py:258
  87.1 0.0 copy-start.7
  87.1 1.0 %copy-done.7 = f32[512,256]{1,0:T(8,128)S(1)} copy-done((f32[512,256]{1,0:T(8,128)S(1)}, f32[512,256]{1,0:T(8,128)}, u32[]{:S(2)}) %copy-start.7) | copy-done | bytes 524312
  88.2 1.5 %final.1 = (bf16[1,512,256]{2,1,0:T(8,128)(2,1)}, bf16[1,512,256]{2,1,0:T(8,128)(2,1)}, bf16[1,512,256]{2,1,0:T(8,128)(2,1)}) custom-call(f32[1,256]{1,0:T(1,128)S(1)} %bitcast.5, f32[512,128]{1,0:T(8,128)S(1)} %get-tuple-element.15.cos_ref, f32[512,128]{1,0:T(8,128)S(1)} %get-tuple-element.16.sin_ref, bf16[512,256]{1,0:T(8,128)(2,1)S(1)} %get-tuple-element.17.krot_ref, ...), custom_call_target="tpu_custom_call" | custom-call | tf_op jit(solution)/shard_map/final/pallas_call | solution.py:242
Async XLA Ops:
  1.3 1.0 %copy-start = (bf16[1,512,256]{2,1,0:T(8,128)(2,1)S(1)}, bf16[1,512,256]{2,1,0:T(8,128)(2,1)}, u32[]{:S(2)}) copy-start(bf16[1,512,256]{2,1,0:T(8,128)(2,1)} %v_ref.5) | copy-start | bytes 786436
  2.2 0.9 %copy-start.2 = (bf16[1,512,256]{2,1,0:T(8,128)(2,1)S(1)}, bf16[1,512,256]{2,1,0:T(8,128)(2,1)}, u32[]{:S(2)}) copy-start(bf16[1,512,256]{2,1,0:T(8,128)(2,1)} %g_ref.5) | copy-start | bytes 786436
  3.2 0.9 %copy-start.4 = (bf16[1,512,256]{2,1,0:T(8,128)(2,1)S(1)}, bf16[1,512,256]{2,1,0:T(8,128)(2,1)}, u32[]{:S(2)}) copy-start(bf16[1,512,256]{2,1,0:T(8,128)(2,1)} %q_ref.3) | copy-start | bytes 786436
  4.1 0.9 %copy-start.8 = (bf16[1,512,256]{2,1,0:T(8,128)(2,1)S(1)}, bf16[1,512,256]{2,1,0:T(8,128)(2,1)}, u32[]{:S(2)}) copy-start(bf16[1,512,256]{2,1,0:T(8,128)(2,1)} %k_ref.1) | copy-start | bytes 786436
  5.1 0.9 copy-start.9
  6.0 0.9 copy-start.10
  8.4 17.3 %copy-start.1 = (bf16[1,512,256]{2,1,0:T(8,128)(2,1)S(1)}, bf16[1,512,256]{2,1,0:T(8,128)(2,1)}, u32[]{:S(2)}) copy-start(bf16[1,512,256]{2,1,0:T(8,128)(2,1)} %v_ref.5) | copy-start | bytes 786436
  8.4 17.3 %copy-start.3 = (bf16[1,512,256]{2,1,0:T(8,128)(2,1)S(1)}, bf16[1,512,256]{2,1,0:T(8,128)(2,1)}, u32[]{:S(2)}) copy-start(bf16[1,512,256]{2,1,0:T(8,128)(2,1)} %g_ref.5) | copy-start | bytes 786436
  8.4 17.3 %copy-start.5 = (bf16[1,512,256]{2,1,0:T(8,128)(2,1)S(1)}, bf16[1,512,256]{2,1,0:T(8,128)(2,1)}, u32[]{:S(2)}) copy-start(bf16[1,512,256]{2,1,0:T(8,128)(2,1)} %q_ref.3) | copy-start | bytes 786436
  8.4 34.4 %all-to-all-start = ((f32[64,16,128]{2,1,0:T(8,128)}), f32[64,16,128]{2,1,0:T(8,128)S(1)}, u32[]{:S(2)}, u32[]{:S(2)}) async-start(f32[64,16,128]{2,1,0:T(8,128)} %get-tuple-element.21), calls=%async_computation | async-start | bytes 1048576 | tf_op jit(solution)/shard_map/all_to_all | solution.py:210
  25.7 0.7 copy-start.11
  28.2 0.8 copy-start.6
  87.1 1.0 %copy-start.7 = (f32[512,256]{1,0:T(8,128)S(1)}, f32[512,256]{1,0:T(8,128)}, u32[]{:S(2)}) copy-start(f32[512,256]{1,0:T(8,128)} %copy-done.6) | copy-start | bytes 1572868

commit v2 on v1

--- a/solution.py
+++ b/solution.py
@@ -16,7 +16,8 @@
 LOW, MIDDLE, HIGH = 32, 64, 65
 TABLE = HIGH + MIDDLE + LOW
 TABLE_ROWS = 168
-PIECE = 16
+SEND = 12
+BACK = 10
 
 
 def rotary_tables():
@@ -39,7 +40,23 @@
     return pltpu.roll(x, HALF, 1)
 
 
-def states_kernel(off_ref, ctab_ref, stab_ref, q_ref, k_ref, v_ref, g_ref, send_ref, krot_ref, cos_ref, sin_ref):
+def states_kernel(
+    off_ref, ctab_hbm, stab_hbm, q_hbm, k_hbm, v_hbm, g_hbm, send_ref, krot_ref, cos_ref, sin_ref,
+    ctab_ref, stab_ref, q_ref, k_ref, v_ref, g_ref, sems,
+):
+    pairs = (
+        (ctab_hbm, ctab_ref),
+        (stab_hbm, stab_ref),
+        (k_hbm, k_ref),
+        (v_hbm, v_ref),
+        (q_hbm, q_ref),
+        (g_hbm, g_ref),
+    )
+    copies = [pltpu.make_async_copy(src, dst, sems.at[i]) for i, (src, dst) in enumerate(pairs)]
+    for copy in copies:
+        copy.start()
+    for copy in copies[:2]:
+        copy.wait()
     offset = off_ref[0, 0]
     high, middle, low = offset // 2048, (offset // 32) % 64, offset % 32
 
@@ -61,13 +78,15 @@
         cos_ref[block * LOW : (block + 1) * LOW, :] = cosine
         sin_ref[block * LOW : (block + 1) * LOW, :] = sine
     cosine, sine = cos_ref[...], sin_ref[...]
+    for copy in copies[2:]:
+        copy.wait()
     for head in range(HEADS):
         lanes = slice(head * DIM, (head + 1) * DIM)
-        q = q_ref[0, :, lanes].astype(jnp.float32)
         k = k_ref[0, :, lanes].astype(jnp.float32)
         krot = (k * cosine + swap(k) * sine).astype(jnp.bfloat16)
         krot_ref[:, lanes] = krot
         kv = dot(krot, v_ref[0, :, lanes], 0, 0)
+        q = q_ref[0, :, lanes].astype(jnp.float32)
         g = g_ref[0, :, lanes]
         qcos = dot((q * cosine).astype(jnp.bfloat16), g, 0, 0)
         qsin = dot((q * -sine).astype(jnp.bfloat16), g, 0, 0)
@@ -75,10 +94,9 @@
             at = 2 * head + half
             rows = slice(half * HALF, (half + 1) * HALF)
             other = slice((1 - half) * HALF, (2 - half) * HALF)
-            send_ref[:, at, :] = kv[rows]
-            send_ref[:, 4 + at, :] = kv[rows]
-            send_ref[:, 8 + at, :] = qcos[rows]
-            send_ref[:, 12 + at, :] = qsin[other]
+            send_ref[pl.ds(at, HALF, stride=SEND), :] = kv[rows]
+            send_ref[pl.ds(4 + at, HALF, stride=SEND), :] = qcos[rows]
+            send_ref[pl.ds(8 + at, HALF, stride=SEND), :] = qsin[other]
 
 
 def local_kernel(
@@ -108,8 +126,7 @@
         part_ref[head : head + 1, :] = jnp.sum(dq * q, axis=0, keepdims=True)
 
 
-def scan_kernel(scale, axis, gain_ref, recv_ref, part_ref, send_ref):
-    count = recv_ref.shape[0]
+def scan_kernel(scale, axis, count, gain_ref, recv_ref, part_ref, send_ref):
     mine = lax.axis_index(axis)
     rows = lax.broadcasted_iota(jnp.int32, (8, DIM), 0)
     gains = [gain_ref[half * HALF + mine] for half in range(4)]
@@ -120,15 +137,16 @@
     before = jnp.zeros((8, DIM), jnp.float32)
     products = jnp.zeros((8, DIM), jnp.float32)
     for shard in range(count):
-        send_ref[shard, 0:8, :] = before
-        products += before * recv_ref[shard, 8:16, :]
-        before += recv_ref[shard, 0:8, :]
+        twice = jnp.where(rows < 4, before, pltpu.roll(before, 4, 0))
+        send_ref[BACK * shard : BACK * shard + 8, :] = twice
+        products += twice * recv_ref[SEND * shard + 4 : SEND * shard + 12, :]
+        before += recv_ref[SEND * shard : SEND * shard + 8, :]
     after = jnp.zeros((8, DIM), jnp.float32)
     for shard in reversed(range(count)):
         back = after * weight
         back = back + pltpu.roll(back, 4, 0)
-        send_ref[shard, 0:8, :] = jnp.where(rows < 4, send_ref[shard, 0:8, :], back)
-        after += recv_ref[shard, 8:16, :]
+        send_ref[BACK * shard + 4 : BACK * shard + 8, :] = back[:4]
+        after += recv_ref[SEND * shard + 4 : SEND * shard + 12, :]
 
     sums = scale * jnp.sum(products, axis=1, keepdims=True)
     lane = lax.broadcasted_iota(jnp.int32, (8, DIM), 1)
@@ -141,25 +159,30 @@
             hit = (rows == head) & (lane == mine + half * HALF)
             part = part + jnp.where(hit, value, 0.0)
     for shard in range(count):
-        send_ref[shard, 8:16, :] = part
-
-
-def gain_kernel(recv_ref, out_ref):
-    out_ref[...] = jnp.sum(recv_ref[:, 8:16, :], axis=0)
+        send_ref[BACK * shard + 8 : BACK * shard + 10, :] = part[:HEADS]
+
+
+def gain_kernel(count, recv_ref, out_ref):
+    copies = out_ref.shape[0] // HEADS
+    for head in range(HEADS):
+        part = jnp.sum(recv_ref[pl.ds(8 + head, count, stride=BACK), :], axis=0, keepdims=True)
+        for copy in range(copies):
+            out_ref[HEADS * copy + head : HEADS * copy + head + 1, :] = part
 
 
 def final_kernel(
-    scale, gain_ref, cos_ref, sin_ref, krot_ref, v_ref, g_ref, dq_ref, dk_ref, dv_ref, recv_ref,
-    gq_ref, gk_ref, gv_ref,
+    scale, factor, gain_ref, cos_ref, sin_ref, krot_ref, v_ref, g_ref, dq_ref, dk_ref, dv_ref, recv_ref, parts_ref,
+    gq_ref, gk_ref, gv_ref, total_ref,
 ):
     cosine, sine = cos_ref[...], sin_ref[...]
     for head in range(HEADS):
         lanes = slice(head * DIM, (head + 1) * DIM)
+        parts = parts_ref[pl.ds(head, parts_ref.shape[0] // HEADS, stride=HEADS), :]
+        total_ref[:, lanes] = jnp.sum(parts, axis=0, keepdims=True) * factor
 
         def matrix(first):
-            return jnp.concatenate(
-                [recv_ref[:, first, :], recv_ref[:, first + 1, :]], axis=0
-            ).astype(jnp.bfloat16)
+            halves = [recv_ref[pl.ds(first + half, HALF, stride=BACK), :] for half in range(2)]
+            return jnp.concatenate(halves, axis=0).astype(jnp.bfloat16)
 
         state = matrix(2 * head)
         back = matrix(4 + 2 * head)
@@ -172,42 +195,61 @@
         gv_ref[0, :, lanes] = (dv_ref[:, lanes] + dv).astype(jnp.bfloat16)
 
 
-def total_kernel(factor, parts_ref, out_ref):
-    out_ref[...] = jnp.sum(parts_ref[...], axis=0) * factor
-
-
 VMEM = pl.BlockSpec(memory_space=pltpu.VMEM)
 SMEM = pl.BlockSpec(memory_space=pltpu.SMEM)
-PARAMS = pltpu.CompilerParams(vmem_limit_bytes=40 * 1024 * 1024)
+HBM = pl.BlockSpec(memory_space=pltpu.HBM)
+PARAMS = pltpu.CompilerParams(vmem_limit_bytes=24 * 1024 * 1024)
 
 
 def shape(*dims, dtype=jnp.float32):
     return jax.ShapeDtypeStruct(dims, dtype)
 
 
+def exchange(rows, axis):
+    count = lax.axis_size(axis)
+    pieces = rows.reshape(count, 1, rows.size // count)
+    return lax.all_to_all(pieces, axis, 0, 0, tiled=True).reshape(rows.shape)
+
+
 def local(queries, keys, values, out_grad, q_gain, offsets):
     rows, width = queries.shape[1], queries.shape[2]
-    shards = lax.axis_size("ctx")
-    all_tokens = rows * shards * lax.axis_size("dp")
+    shards, groups = lax.axis_size("ctx"), lax.axis_size("dp")
     scale = float((DIM * rows * shards) ** (-0.5))
+    factor = float((rows * shards * groups) ** (-0.5))
     cos_table, sin_table = rotary_tables()
     gain_row = q_gain.reshape(1, width)
+    tokens = queries.shape
 
     sent, krot, cosine, sine = pl.pallas_call(
         states_kernel,
         out_shape=(
-            shape(shards, PIECE, DIM),
+            shape(shards * SEND, DIM),
             shape(rows, width, dtype=jnp.bfloat16),
             shape(rows, DIM),
             shape(rows, DIM),
         ),
-        in_specs=[SMEM] + [VMEM] * 6,
+        in_specs=[SMEM] + [HBM] * 6,
         out_specs=(VMEM,) * 4,
+        scratch_shapes=[
+            pltpu.VMEM(cos_table.shape, jnp.float32),
+            pltpu.VMEM(cos_table.shape, jnp.float32),
+            pltpu.VMEM(tokens, jnp.bfloat16),
+            pltpu.VMEM(tokens, jnp.bfloat16),
+            pltpu.VMEM(tokens, jnp.bfloat16),
+            pltpu.VMEM(tokens, jnp.bfloat16),
+            pltpu.SemaphoreType.DMA((6,)),
+        ],
         compiler_params=PARAMS,
         name="states",
-    )(offsets, jnp.asarray(cos_table), jnp.asarray(sin_table), queries, keys, values, out_grad)
-
-    received = lax.all_to_all(sent, "ctx", 0, 0, tiled=True)
+    )(
+        offsets,
+        *(
+            pltpu.with_memory_space_constraint(x, pltpu.HBM)
+            for x in (jnp.asarray(cos_table), jnp.asarray(sin_table), queries, keys, values, out_grad)
+        )
+    )
+
+    received = exchange(sent, "ctx")
 
     dq, dk, dv, part = pl.pallas_call(
         functools.partial(local_kernel, scale),
@@ -219,44 +261,35 @@
     )(gain_row, cosine, sine, queries, krot, values, out_grad)
 
     scanned = pl.pallas_call(
-        functools.partial(scan_kernel, scale, "ctx"),
-        out_shape=shape(shards, PIECE, DIM),
+        functools.partial(scan_kernel, scale, "ctx", shards),
+        out_shape=shape(shards * BACK, DIM),
         in_specs=[SMEM, VMEM, VMEM],
         out_specs=VMEM,
         compiler_params=PARAMS,
         name="scan",
     )(q_gain, received, part)
 
-    states = lax.all_to_all(scanned, "ctx", 0, 0, tiled=True)
+    states = exchange(scanned, "ctx")
 
     gain_part = pl.pallas_call(
-        gain_kernel,
-        out_shape=shape(8, DIM),
+        functools.partial(gain_kernel, shards),
+        out_shape=shape(groups * HEADS, DIM),
         in_specs=[VMEM],
         out_specs=VMEM,
         compiler_params=PARAMS,
         name="gain_part",
     )(states)
-    gathered = lax.all_gather(gain_part, "dp")
-
-    grad_queries, grad_keys, grad_values = pl.pallas_call(
-        functools.partial(final_kernel, scale),
-        out_shape=(shape(1, rows, width, dtype=jnp.bfloat16),) * 3,
-        in_specs=[VMEM] * 10,
-        out_specs=(VMEM,) * 3,
+    gain_parts = exchange(gain_part, "dp")
+
+    grad_queries, grad_keys, grad_values, grad_gain = pl.pallas_call(
+        functools.partial(final_kernel, scale, factor),
+        out_shape=(shape(*tokens, dtype=jnp.bfloat16),) * 3 + (shape(1, width),),
+        in_specs=[VMEM] * 11,
+        out_specs=(VMEM,) * 4,
         compiler_params=PARAMS,
         name="final",
-    )(gain_row, cosine, sine, krot, values, out_grad, dq, dk, dv, states)
-
-    total = pl.pallas_call(
-        functools.partial(total_kernel, float(all_tokens ** (-0.5))),
-        out_shape=shape(8, DIM),
-        in_specs=[VMEM],
-        out_specs=VMEM,
-        name="gain_total",
-    )(gathered)
-    grad_gain = total[:HEADS].reshape(width)
-    return grad_queries, grad_keys, grad_values, grad_gain
+    )(gain_row, cosine, sine, krot, values, out_grad, dq, dk, dv, states, gain_parts)
+    return grad_queries, grad_keys, grad_values, grad_gain.reshape(width)
 
 
 def solution(mesh):

time: 90.2 us -> 70.4 us (0.78)
  blocking collectives: 40.8 us -> 31.6 us
  local copies, waits for them, and re-layouts: 9.3 us -> 0.66 us
  waiting for transfers between devices: 13.9 us -> 12.6 us
    all_gather x1 -> x0, blocking collectives: 18.4 us -> none  [local(): gathered = lax.all_gather(gain_part, 'dp')]
    all_to_all x1 -> x2, blocking collectives: 22.4 us -> 31.6 us  [exchange(): return lax.all_to_all(pieces, axis, 0, 0, tiled=True).reshape(rows.shape)]
    unnamed x24 -> x8, local copies, waits for them, and re-layouts: 8.05 us -> 0.66 us
    all_to_all x1, waiting for transfers between devices: 13.9 us -> 12.6 us  [exchange(): return lax.all_to_all(pieces, axis, 0, 0, tiled=True).reshape(rows.shape)]
    reshape x1 -> x0, local copies, waits for them, and re-layouts: 1.25 us -> none  [local(): grad_gain = total[:HEADS].reshape(width)]
    pallas_call x5 -> x4, Pallas kernels: 5.23 us -> 4.83 us  [the longest x1 2.66 us: local(): pl.pallas_call(states_kernel, out_shape=(shape(shards * SEND, DIM), shape...]
  transfers between devices with their start and end apart: 1 -> 1, of which waited for: 1 -> 1; matrix products, arithmetic and copies ran while one was open for 0% -> 0% of each run, Pallas kernels for 2% -> 3%
where the time goes in v2:
time: 70.4 us; the launch traced here: 70.1 us
  blocking collectives  31.6 us (45%)
  starting transfers between devices  17.3 us (25%)
  waiting for transfers between devices  12.6 us (18%)
  Pallas kernels  6.61 us (9%)
  between operations  1.37 us (2%)
    all_to_all x2, blocking collectives, exchange(): return lax.all_to_all(pieces, axis, 0, 0, tiled=True).reshape(rows.shape)  31.6 us
    all_to_all x1, starting transfers between devices, exchange(): return lax.all_to_all(pieces, axis, 0, 0, tiled=True).reshape(rows.shape)  17.3 us
    all_to_all x1, waiting for transfers between devices, exchange(): return lax.all_to_all(pieces, axis, 0, 0, tiled=True).reshape(rows.shape)  12.6 us
    pallas_call x1, Pallas kernels, local(): pl.pallas_call(states_kernel, out_shape=(shape(shards * SEND, DIM), shape...  2.66 us
    pallas_call x1, Pallas kernels, local(): pl.pallas_call(functools.partial(local_kernel, scale), out_shape=(shape(r...  1.78 us
  transfers between devices with their start and end apart: 1, of which 1 were waited for; matrix products, arithmetic and copies ran while one was open for 0% of the time, Pallas kernels for 3%

profile of v2, /device:TPU:1, one launch (start us, length us, event | category | flops | bytes accessed | tf_op | source)
XLA Modules:
  0.0 70.1 jit_solution(8283939068488939411)
XLA Ops:
  1.3 2.7 %states.1 = (f32[768,128]{1,0:T(8,128)}, bf16[512,256]{1,0:T(8,128)(2,1)S(1)}, f32[512,128]{1,0:T(8,128)S(1)}, f32[512,128]{1,0:T(8,128)S(1)}) custom-call(s32[1,1]{1,0:T(1,128)S(6)} %copy.15.off_ref, f32[168,128]{1,0:T(8,128)} %constant.4.clone.ctab_hbm, f32[168,128]{1,0:T(8,128)} %constant.5.clone.stab_hbm, bf16[1,512,256]{2,1,0:T(8,128)(2,1)} %q_ref.1, ...), custom_call_target="tpu_custom_call" | custom-call | tf_op jit(solution)/shard_map/states/pallas_call | solution.py:223
  3.9 0.0 copy-start
  4.0 0.0 copy-start.1
  4.0 0.0 copy-start.2
  4.0 17.3 %all-to-all-start = ((f32[64,1,1536]{2,1,0:T(1,128)}), f32[64,1,1536]{2,1,0:T(1,128)S(1)}, u32[]{:S(2)}, u32[]{:S(2)}) async-start(f32[64,1,1536]{2,1,0:T(1,128)} %bitcast.1), calls=%async_computation | async-start | bytes 786432 | tf_op jit(solution)/shard_map/all_to_all | solution.py:211
  21.3 0.0 copy-start.3
  21.3 0.0 copy-done
  21.3 0.0 copy-done.1
  21.3 0.0 copy-done.2
  21.3 0.6 copy-done.3
  22.0 1.8 %local_grads.1 = (f32[512,256]{1,0:T(8,128)S(1)}, f32[512,256]{1,0:T(8,128)S(1)}, f32[512,256]{1,0:T(8,128)S(1)}, f32[8,128]{1,0:T(8,128)S(1)}) custom-call(f32[1,256]{1,0:T(1,128)S(1)} %bitcast.14, f32[512,128]{1,0:T(8,128)S(1)} %get-tuple-element.16.cos_ref, f32[512,128]{1,0:T(8,128)S(1)} %get-tuple-element.17.sin_ref, bf16[1,512,256]{2,1,0:T(8,128)(2,1)S(1)} %copy-done.2, ...), custom_call_target="tpu_custom_call" | custom-call | tf_op jit(solution)/shard_map/local_grads/pallas_call | solution.py:254
  23.7 12.6 %all-to-all-done = f32[64,1,1536]{2,1,0:T(1,128)S(1)} async-done(((f32[64,1,1536]{2,1,0:T(1,128)}), f32[64,1,1536]{2,1,0:T(1,128)S(1)}, u32[]{:S(2)}, u32[]{:S(2)}) %all-to-all-start) | async-done | bytes 393248 | tf_op jit(solution)/shard_map/all_to_all | solution.py:211
  36.3 0.8 %scan.1 = f32[640,128]{1,0:T(8,128)S(1)} custom-call(f32[256]{0:T(256)S(1)} %copy-done.3, f32[768,128]{1,0:T(8,128)S(1)} %bitcast.10, f32[8,128]{1,0:T(8,128)S(1)} %get-tuple-element.23.part_ref), custom_call_target="tpu_custom_call" | custom-call | tf_op jit(solution)/shard_map/scan/pallas_call | solution.py:263
  37.1 18.8 %all_to_all.15 = f32[64,1,1280]{2,1,0:T(1,128)S(1)} all-to-all(f32[64,1,1280]{2,1,0:T(1,128)S(1)} %bitcast.11), channel_id=1, replica_groups=mesh['dp'=8,'ctx'=64] {'ctx'}, dimensions={0} | all-to-all | bytes 655360 | tf_op jit(solution)/shard_map/all_to_all | solution.py:211
  55.9 12.8 %all_to_all.16 = f32[8,1,256]{2,1,0:T(1,128)S(1)} all-to-all(f32[8,1,256]{2,1,0:T(1,128)S(1)} %bitcast.13), channel_id=1, replica_groups=mesh['dp'=8,'ctx'=64] {'dp'}, dimensions={0} | all-to-all | bytes 16384 | tf_op jit(solution)/shard_map/all_to_all | solution.py:211
  68.7 1.4 %final.1 = (bf16[1,512,256]{2,1,0:T(8,128)(2,1)}, bf16[1,512,256]{2,1,0:T(8,128)(2,1)}, bf16[1,512,256]{2,1,0:T(8,128)(2,1)}, f32[1,256]{1,0:T(1,128)}) custom-call(f32[1,256]{1,0:T(1,128)S(1)} %bitcast.15, f32[512,128]{1,0:T(8,128)S(1)} %get-tuple-element.16.cos_ref, f32[512,128]{1,0:T(8,128)S(1)} %get-tuple-element.17.sin_ref, ...), custom_call_target="tpu_custom_call" | custom-call | tf_op jit(solution)/shard_map/final/pallas_call | solution.py:284
  (1 shorter events, 0.0 us)
Async XLA Ops:
  3.9 17.3 %copy-start = (bf16[1,512,256]{2,1,0:T(8,128)(2,1)S(1)}, bf16[1,512,256]{2,1,0:T(8,128)(2,1)}, u32[]{:S(2)}) copy-start(bf16[1,512,256]{2,1,0:T(8,128)(2,1)} %v_ref.3) | copy-start | bytes 786436
  4.0 17.3 %copy-start.1 = (bf16[1,512,256]{2,1,0:T(8,128)(2,1)S(1)}, bf16[1,512,256]{2,1,0:T(8,128)(2,1)}, u32[]{:S(2)}) copy-start(bf16[1,512,256]{2,1,0:T(8,128)(2,1)} %g_ref.3) | copy-start | bytes 786436
  4.0 17.3 %copy-start.2 = (bf16[1,512,256]{2,1,0:T(8,128)(2,1)S(1)}, bf16[1,512,256]{2,1,0:T(8,128)(2,1)}, u32[]{:S(2)}) copy-start(bf16[1,512,256]{2,1,0:T(8,128)(2,1)} %q_ref.1) | copy-start | bytes 786436
  4.0 32.3 %all-to-all-start = ((f32[64,1,1536]{2,1,0:T(1,128)}), f32[64,1,1536]{2,1,0:T(1,128)S(1)}, u32[]{:S(2)}, u32[]{:S(2)}) async-start(f32[64,1,1536]{2,1,0:T(1,128)} %bitcast.1), calls=%async_computation | async-start | bytes 786432 | tf_op jit(solution)/shard_map/all_to_all | solution.py:211
  21.3 0.7 copy-start.3

commit v3 on v2

--- a/solution.py
+++ b/solution.py
@@ -18,6 +18,8 @@
 TABLE_ROWS = 168
 SEND = 12
 BACK = 10
+SIDE = 8
+FIRST = (5, 4)
 
 
 def rotary_tables():
@@ -126,8 +128,15 @@
         part_ref[head : head + 1, :] = jnp.sum(dq * q, axis=0, keepdims=True)
 
 
+def rank(shard):
+    return (shard // SIDE - FIRST[0]) % SIDE * SIDE + (shard % SIDE - FIRST[1]) % SIDE
+
+
 def scan_kernel(scale, axis, count, gain_ref, recv_ref, part_ref, send_ref):
-    mine = lax.axis_index(axis)
+    index = lax.axis_index(axis)
+    mine = lax.rem(lax.div(index, SIDE) + SIDE - FIRST[0], SIDE) * SIDE + lax.rem(
+        lax.rem(index, SIDE) + SIDE - FIRST[1], SIDE
+    )
     rows = lax.broadcasted_iota(jnp.int32, (8, DIM), 0)
     gains = [gain_ref[half * HALF + mine] for half in range(4)]
     weight = jnp.zeros((8, DIM), jnp.float32)
@@ -137,16 +146,18 @@
     before = jnp.zeros((8, DIM), jnp.float32)
     products = jnp.zeros((8, DIM), jnp.float32)
     for shard in range(count):
+        source, target = SEND * rank(shard), BACK * rank(shard)
         twice = jnp.where(rows < 4, before, pltpu.roll(before, 4, 0))
-        send_ref[BACK * shard : BACK * shard + 8, :] = twice
-        products += twice * recv_ref[SEND * shard + 4 : SEND * shard + 12, :]
-        before += recv_ref[SEND * shard : SEND * shard + 8, :]
+        send_ref[target : target + 8, :] = twice
+        products += twice * recv_ref[source + 4 : source + 12, :]
+        before += recv_ref[source : source + 8, :]
     after = jnp.zeros((8, DIM), jnp.float32)
     for shard in reversed(range(count)):
+        source, target = SEND * rank(shard), BACK * rank(shard)
         back = after * weight
         back = back + pltpu.roll(back, 4, 0)
-        send_ref[BACK * shard + 4 : BACK * shard + 8, :] = back[:4]
-        after += recv_ref[SEND * shard + 4 : SEND * shard + 12, :]
+        send_ref[target + 4 : target + 8, :] = back[:4]
+        after += recv_ref[source + 4 : source + 12, :]
 
     sums = scale * jnp.sum(products, axis=1, keepdims=True)
     lane = lax.broadcasted_iota(jnp.int32, (8, DIM), 1)
@@ -205,10 +216,11 @@
     return jax.ShapeDtypeStruct(dims, dtype)
 
 
-def exchange(rows, axis):
+def exchange(rows, axis, order=None):
     count = lax.axis_size(axis)
     pieces = rows.reshape(count, 1, rows.size // count)
-    return lax.all_to_all(pieces, axis, 0, 0, tiled=True).reshape(rows.shape)
+    groups = None if order is None else [order]
+    return lax.all_to_all(pieces, axis, 0, 0, axis_index_groups=groups, tiled=True).reshape(rows.shape)
 
 
 def local(queries, keys, values, out_grad, q_gain, offsets):
@@ -218,6 +230,7 @@
     factor = float((rows * shards * groups) ** (-0.5))
     cos_table, sin_table = rotary_tables()
     gain_row = q_gain.reshape(1, width)
+    order = sorted(range(shards), key=rank)
     tokens = queries.shape
 
     sent, krot, cosine, sine = pl.pallas_call(
@@ -249,7 +262,7 @@
         )
     )
 
-    received = exchange(sent, "ctx")
+    received = exchange(sent, "ctx", order)
 
     dq, dk, dv, part = pl.pallas_call(
         functools.partial(local_kernel, scale),
@@ -269,7 +282,7 @@
         name="scan",
     )(q_gain, received, part)
 
-    states = exchange(scanned, "ctx")
+    states = exchange(scanned, "ctx", order)
 
     gain_part = pl.pallas_call(
         functools.partial(gain_kernel, shards),

time: 70.4 us -> 65.3 us (0.928)
  waiting for transfers between devices: 12.6 us -> 6.73 us
  starting transfers between devices: 17.3 us -> 19.3 us
  blocking collectives: 31.6 us -> 30.3 us
    all_to_all x1, waiting for transfers between devices: 12.6 us -> 6.73 us  [exchange(): lax.all_to_all(pieces, axis, 0, 0, axis_index_groups=groups, tiled=True)]
    all_to_all x1, starting transfers between devices: 17.3 us -> 19.3 us  [exchange(): lax.all_to_all(pieces, axis, 0, 0, axis_index_groups=groups, tiled=True)]
    all_to_all x2, blocking collectives: 31.6 us -> 30.3 us  [exchange(): lax.all_to_all(pieces, axis, 0, 0, axis_index_groups=groups, tiled=True)]
where the time goes in v3:
time: 65.3 us; the launch traced here: 65 us
  blocking collectives  30.3 us (46%)
  starting transfers between devices  19.3 us (30%)
  waiting for transfers between devices  6.73 us (10%)
  Pallas kernels  6.61 us (10%)
  between operations  1.37 us (2%)
  local copies, waits for them, and re-layouts  0.66 us (1%)
    all_to_all x2, blocking collectives, exchange(): lax.all_to_all(pieces, axis, 0, 0, axis_index_groups=groups, tiled=True)  30.3 us
    all_to_all x1, starting transfers between devices, exchange(): lax.all_to_all(pieces, axis, 0, 0, axis_index_groups=groups, tiled=True)  19.3 us
    all_to_all x1, waiting for transfers between devices, exchange(): lax.all_to_all(pieces, axis, 0, 0, axis_index_groups=groups, tiled=True)  6.73 us
    pallas_call x1, Pallas kernels, local(): pl.pallas_call(states_kernel, out_shape=(shape(shards * SEND, DIM), shape...  2.66 us
    pallas_call x1, Pallas kernels, local(): pl.pallas_call(functools.partial(local_kernel, scale), out_shape=(shape(r...  1.78 us
    pallas_call x1, Pallas kernels, local(): pl.pallas_call(functools.partial(final_kernel, scale, factor), out_shape=...  1.39 us
  transfers between devices with their start and end apart: 1, of which 1 were waited for; matrix products, arithmetic and copies ran while one was open for 0% of the time, Pallas kernels for 3%

profile of v3, /device:TPU:1, one launch (start us, length us, event | category | flops | bytes accessed | tf_op | source)
XLA Modules:
  0.0 65.0 jit_solution(16069518899718307241)
XLA Ops:
  1.3 2.7 %states.1 = (f32[768,128]{1,0:T(8,128)}, bf16[512,256]{1,0:T(8,128)(2,1)S(1)}, f32[512,128]{1,0:T(8,128)S(1)}, f32[512,128]{1,0:T(8,128)S(1)}) custom-call(s32[1,1]{1,0:T(1,128)S(6)} %copy.15.off_ref, f32[168,128]{1,0:T(8,128)} %constant.4.clone.ctab_hbm, f32[168,128]{1,0:T(8,128)} %constant.5.clone.stab_hbm, bf16[1,512,256]{2,1,0:T(8,128)(2,1)} %q_ref.1, ...), custom_call_target="tpu_custom_call" | custom-call | tf_op jit(solution)/shard_map/states/pallas_call | solution.py:236
  3.9 0.0 copy-start
  4.0 0.0 copy-start.1
  4.0 0.0 copy-start.2
  4.0 19.3 %all-to-all-start = ((f32[64,1,1536]{2,1,0:T(1,128)}), f32[64,1,1536]{2,1,0:T(1,128)S(1)}, u32[]{:S(2)}, u32[]{:S(2)}) async-start(f32[64,1,1536]{2,1,0:T(1,128)} %bitcast.1), calls=%async_computation | async-start | bytes 786432 | tf_op jit(solution)/shard_map/all_to_all | solution.py:223
  23.3 0.0 copy-start.3
  23.3 0.0 copy-done
  23.3 0.0 copy-done.1
  23.3 0.0 copy-done.2
  23.4 0.6 copy-done.3
  24.0 1.8 %local_grads.1 = (f32[512,256]{1,0:T(8,128)S(1)}, f32[512,256]{1,0:T(8,128)S(1)}, f32[512,256]{1,0:T(8,128)S(1)}, f32[8,128]{1,0:T(8,128)S(1)}) custom-call(f32[1,256]{1,0:T(1,128)S(1)} %bitcast.14, f32[512,128]{1,0:T(8,128)S(1)} %get-tuple-element.16.cos_ref, f32[512,128]{1,0:T(8,128)S(1)} %get-tuple-element.17.sin_ref, bf16[1,512,256]{2,1,0:T(8,128)(2,1)S(1)} %copy-done.2, ...), custom_call_target="tpu_custom_call" | custom-call | tf_op jit(solution)/shard_map/local_grads/pallas_call | solution.py:267
  25.8 6.7 %all-to-all-done = f32[64,1,1536]{2,1,0:T(1,128)S(1)} async-done(((f32[64,1,1536]{2,1,0:T(1,128)}), f32[64,1,1536]{2,1,0:T(1,128)S(1)}, u32[]{:S(2)}, u32[]{:S(2)}) %all-to-all-start) | async-done | bytes 393248 | tf_op jit(solution)/shard_map/all_to_all | solution.py:223
  32.5 0.8 %scan.1 = f32[640,128]{1,0:T(8,128)S(1)} custom-call(f32[256]{0:T(256)S(1)} %copy-done.3, f32[768,128]{1,0:T(8,128)S(1)} %bitcast.10, f32[8,128]{1,0:T(8,128)S(1)} %get-tuple-element.23.part_ref), custom_call_target="tpu_custom_call" | custom-call | tf_op jit(solution)/shard_map/scan/pallas_call | solution.py:276
  33.3 18.8 %all_to_all.15 = f32[64,1,1280]{2,1,0:T(1,128)S(1)} all-to-all(f32[64,1,1280]{2,1,0:T(1,128)S(1)} %bitcast.11), channel_id=1, replica_groups={{44,45,46,47,40,41,42,43,52,53,54,55,48,49,50,51,60,61,62,63,56,57,58,5..., dimensions={0} | all-to-all | bytes 655360 | tf_op jit(solution)/shard_map/all_to_all | solution.py:223
  52.1 11.5 %all_to_all.16 = f32[8,1,256]{2,1,0:T(1,128)S(1)} all-to-all(f32[8,1,256]{2,1,0:T(1,128)S(1)} %bitcast.13), channel_id=1, replica_groups=mesh['dp'=8,'ctx'=64] {'dp'}, dimensions={0} | all-to-all | bytes 16384 | tf_op jit(solution)/shard_map/all_to_all | solution.py:223
  63.6 1.4 %final.1 = (bf16[1,512,256]{2,1,0:T(8,128)(2,1)}, bf16[1,512,256]{2,1,0:T(8,128)(2,1)}, bf16[1,512,256]{2,1,0:T(8,128)(2,1)}, f32[1,256]{1,0:T(1,128)}) custom-call(f32[1,256]{1,0:T(1,128)S(1)} %bitcast.15, f32[512,128]{1,0:T(8,128)S(1)} %get-tuple-element.16.cos_ref, f32[512,128]{1,0:T(8,128)S(1)} %get-tuple-element.17.sin_ref, ...), custom_call_target="tpu_custom_call" | custom-call | tf_op jit(solution)/shard_map/final/pallas_call | solution.py:297
  (1 shorter events, 0.0 us)
Async XLA Ops:
  3.9 19.4 %copy-start = (bf16[1,512,256]{2,1,0:T(8,128)(2,1)S(1)}, bf16[1,512,256]{2,1,0:T(8,128)(2,1)}, u32[]{:S(2)}) copy-start(bf16[1,512,256]{2,1,0:T(8,128)(2,1)} %v_ref.3) | copy-start | bytes 786436
  4.0 19.4 %copy-start.1 = (bf16[1,512,256]{2,1,0:T(8,128)(2,1)S(1)}, bf16[1,512,256]{2,1,0:T(8,128)(2,1)}, u32[]{:S(2)}) copy-start(bf16[1,512,256]{2,1,0:T(8,128)(2,1)} %g_ref.3) | copy-start | bytes 786436
  4.0 19.4 %copy-start.2 = (bf16[1,512,256]{2,1,0:T(8,128)(2,1)S(1)}, bf16[1,512,256]{2,1,0:T(8,128)(2,1)}, u32[]{:S(2)}) copy-start(bf16[1,512,256]{2,1,0:T(8,128)(2,1)} %q_ref.1) | copy-start | bytes 786436
  4.0 28.5 %all-to-all-start = ((f32[64,1,1536]{2,1,0:T(1,128)}), f32[64,1,1536]{2,1,0:T(1,128)S(1)}, u32[]{:S(2)}, u32[]{:S(2)}) async-start(f32[64,1,1536]{2,1,0:T(1,128)} %bitcast.1), calls=%async_computation | async-start | bytes 786432 | tf_op jit(solution)/shard_map/all_to_all | solution.py:223
  23.3 0.7 %copy-start.3 = (f32[256]{0:T(256)S(1)}, f32[256]{0:T(256)}, u32[]{:S(2)}) copy-start(f32[256]{0:T(256)} %gain_ref.1) | copy-start | bytes 3076

commit v4 on v3

--- a/solution.py
+++ b/solution.py
@@ -19,7 +19,8 @@
 SEND = 12
 BACK = 10
 SIDE = 8
-FIRST = (5, 4)
+FIRST = (4, 4)
+FIRST_DP = 4
 
 
 def rotary_tables():
@@ -87,18 +88,16 @@
         k = k_ref[0, :, lanes].astype(jnp.float32)
         krot = (k * cosine + swap(k) * sine).astype(jnp.bfloat16)
         krot_ref[:, lanes] = krot
-        kv = dot(krot, v_ref[0, :, lanes], 0, 0)
+        kv = dot(v_ref[0, :, lanes], krot, 0, 0)
         q = q_ref[0, :, lanes].astype(jnp.float32)
-        g = g_ref[0, :, lanes]
-        qcos = dot((q * cosine).astype(jnp.bfloat16), g, 0, 0)
-        qsin = dot((q * -sine).astype(jnp.bfloat16), g, 0, 0)
+        pair = jnp.concatenate([q * cosine, q * -sine], axis=1).astype(jnp.bfloat16)
+        gq = dot(g_ref[0, :, lanes], pair, 0, 0)
         for half in range(2):
             at = 2 * head + half
             rows = slice(half * HALF, (half + 1) * HALF)
-            other = slice((1 - half) * HALF, (2 - half) * HALF)
             send_ref[pl.ds(at, HALF, stride=SEND), :] = kv[rows]
-            send_ref[pl.ds(4 + at, HALF, stride=SEND), :] = qcos[rows]
-            send_ref[pl.ds(8 + at, HALF, stride=SEND), :] = qsin[other]
+            send_ref[pl.ds(4 + at, HALF, stride=SEND), :] = gq[rows, :DIM]
+            send_ref[pl.ds(8 + at, HALF, stride=SEND), :] = gq[rows, DIM:]
 
 
 def local_kernel(
@@ -132,22 +131,15 @@
     return (shard // SIDE - FIRST[0]) % SIDE * SIDE + (shard % SIDE - FIRST[1]) % SIDE
 
 
-def scan_kernel(scale, axis, count, gain_ref, recv_ref, part_ref, send_ref):
-    index = lax.axis_index(axis)
-    mine = lax.rem(lax.div(index, SIDE) + SIDE - FIRST[0], SIDE) * SIDE + lax.rem(
-        lax.rem(index, SIDE) + SIDE - FIRST[1], SIDE
-    )
+def scan_kernel(scale, count, gain_ref, recv_ref, part_ref, send_ref):
     rows = lax.broadcasted_iota(jnp.int32, (8, DIM), 0)
-    gains = [gain_ref[half * HALF + mine] for half in range(4)]
-    weight = jnp.zeros((8, DIM), jnp.float32)
-    for at, source in enumerate((0, 1, 2, 3, 1, 0, 3, 2)):
-        weight = jnp.where(rows == at, gains[source], weight)
+    weight = jnp.where(rows % 4 < 2, gain_ref[:, :DIM], gain_ref[:, DIM:])
 
     before = jnp.zeros((8, DIM), jnp.float32)
     products = jnp.zeros((8, DIM), jnp.float32)
     for shard in range(count):
         source, target = SEND * rank(shard), BACK * rank(shard)
-        twice = jnp.where(rows < 4, before, pltpu.roll(before, 4, 0))
+        twice = jnp.where(rows < 4, before, swap(pltpu.roll(before, 4, 0)))
         send_ref[target : target + 8, :] = twice
         products += twice * recv_ref[source + 4 : source + 12, :]
         before += recv_ref[source : source + 8, :]
@@ -155,20 +147,15 @@
     for shard in reversed(range(count)):
         source, target = SEND * rank(shard), BACK * rank(shard)
         back = after * weight
-        back = back + pltpu.roll(back, 4, 0)
+        back = back + swap(pltpu.roll(back, 4, 0))
         send_ref[target + 4 : target + 8, :] = back[:4]
         after += recv_ref[source + 4 : source + 12, :]
 
-    sums = scale * jnp.sum(products, axis=1, keepdims=True)
-    lane = lax.broadcasted_iota(jnp.int32, (8, DIM), 1)
     part = part_ref[...]
     for head in range(HEADS):
-        for half in range(2):
-            at = 2 * head + half
-            other = 4 + 2 * head + 1 - half
-            value = sums[at : at + 1] + sums[other : other + 1]
-            hit = (rows == head) & (lane == mine + half * HALF)
-            part = part + jnp.where(hit, value, 0.0)
+        mine = jnp.where(rows % 4 // 2 == head, products, 0.0)
+        total = scale * jnp.sum(mine, axis=0, keepdims=True)
+        part = part + jnp.where(rows == head, total, 0.0)
     for shard in range(count):
         send_ref[BACK * shard + 8 : BACK * shard + 10, :] = part[:HEADS]
 
@@ -197,12 +184,12 @@
 
         state = matrix(2 * head)
         back = matrix(4 + 2 * head)
-        dq = scale * dot(g_ref[0, :, lanes], state, 1, 1)
+        dq = scale * dot(g_ref[0, :, lanes], state, 1, 0)
         dq = dq_ref[:, lanes] + (dq * cosine - swap(dq) * sine)
         gq_ref[0, :, lanes] = (dq * gain_ref[:, lanes]).astype(jnp.bfloat16)
-        dk = scale * dot(v_ref[0, :, lanes], back, 1, 1)
+        dk = scale * dot(v_ref[0, :, lanes], back, 1, 0)
         gk_ref[0, :, lanes] = (dk_ref[:, lanes] + (dk * cosine - swap(dk) * sine)).astype(jnp.bfloat16)
-        dv = scale * dot(krot_ref[:, lanes], back, 1, 0)
+        dv = scale * dot(krot_ref[:, lanes], back, 1, 1)
         gv_ref[0, :, lanes] = (dv_ref[:, lanes] + dv).astype(jnp.bfloat16)
 
 
@@ -274,13 +261,13 @@
     )(gain_row, cosine, sine, queries, krot, values, out_grad)
 
     scanned = pl.pallas_call(
-        functools.partial(scan_kernel, scale, "ctx", shards),
+        functools.partial(scan_kernel, scale, shards),
         out_shape=shape(shards * BACK, DIM),
-        in_specs=[SMEM, VMEM, VMEM],
+        in_specs=[VMEM] * 3,
         out_specs=VMEM,
         compiler_params=PARAMS,
         name="scan",
-    )(q_gain, received, part)
+    )(gain_row, received, part)
 
     states = exchange(scanned, "ctx", order)
 
@@ -292,7 +279,7 @@
         compiler_params=PARAMS,
         name="gain_part",
     )(states)
-    gain_parts = exchange(gain_part, "dp")
+    gain_parts = exchange(gain_part, "dp", [(FIRST_DP + i) % groups for i in range(groups)])
 
     grad_queries, grad_keys, grad_values, grad_gain = pl.pallas_call(
         functools.partial(final_kernel, scale, factor),

time: 65.3 us -> 62.7 us (0.960)
  blocking collectives: 30.3 us -> 28.1 us
  starting transfers between devices: 19.3 us -> 20.3 us
  Pallas kernels: 6.61 us -> 5.9 us
    all_to_all x2, blocking collectives: 30.3 us -> 28.1 us  [exchange(): lax.all_to_all(pieces, axis, 0, 0, axis_index_groups=groups, tiled=True)]
    all_to_all x1, starting transfers between devices: 19.3 us -> 20.3 us  [exchange(): lax.all_to_all(pieces, axis, 0, 0, axis_index_groups=groups, tiled=True)]
where the time goes in v4:
time: 62.7 us; the launch traced here: 62.4 us
  blocking collectives  28.1 us (45%)
  starting transfers between devices  20.3 us (32%)
  waiting for transfers between devices  6.09 us (10%)
  Pallas kernels  5.9 us (9%)
  between operations  1.36 us (2%)
  local copies, waits for them, and re-layouts  0.66 us (1%)
    all_to_all x2, blocking collectives, exchange(): lax.all_to_all(pieces, axis, 0, 0, axis_index_groups=groups, tiled=True)  28.1 us
    all_to_all x1, starting transfers between devices, exchange(): lax.all_to_all(pieces, axis, 0, 0, axis_index_groups=groups, tiled=True)  20.3 us
    all_to_all x1, waiting for transfers between devices, exchange(): lax.all_to_all(pieces, axis, 0, 0, axis_index_groups=groups, tiled=True)  6.09 us
    pallas_call x1, Pallas kernels, local(): pl.pallas_call(states_kernel, out_shape=(shape(shards * SEND, DIM), shape...  2.53 us
    pallas_call x1, Pallas kernels, local(): pl.pallas_call(functools.partial(local_kernel, scale), out_shape=(shape(r...  1.78 us
    pallas_call x1, Pallas kernels, local(): pl.pallas_call(functools.partial(final_kernel, scale, factor), out_shape=...  1.37 us
  transfers between devices with their start and end apart: 1, of which 1 were waited for; matrix products, arithmetic and copies ran while one was open for 0% of the time, Pallas kernels for 3%

profile of v4, /device:TPU:1, one launch (start us, length us, event | category | flops | bytes accessed | tf_op | source)
XLA Modules:
  0.0 62.4 jit_solution(14074416100867905731)
XLA Ops:
  1.3 2.5 %states.1 = (f32[768,128]{1,0:T(8,128)}, bf16[512,256]{1,0:T(8,128)(2,1)S(1)}, f32[512,128]{1,0:T(8,128)S(1)}, f32[512,128]{1,0:T(8,128)S(1)}) custom-call(s32[1,1]{1,0:T(1,128)S(6)} %copy.15.off_ref, f32[168,128]{1,0:T(8,128)} %constant.4.clone.ctab_hbm, f32[168,128]{1,0:T(8,128)} %constant.5.clone.stab_hbm, bf16[1,512,256]{2,1,0:T(8,128)(2,1)} %q_ref.1, ...), custom_call_target="tpu_custom_call" | custom-call | tf_op jit(solution)/shard_map/states/pallas_call | solution.py:223
  3.8 0.0 copy-start
  3.8 0.0 copy-start.1
  3.8 0.0 copy-start.2
  3.9 20.3 %all-to-all-start = ((f32[64,1,1536]{2,1,0:T(1,128)}), f32[64,1,1536]{2,1,0:T(1,128)S(1)}, u32[]{:S(2)}, u32[]{:S(2)}) async-start(f32[64,1,1536]{2,1,0:T(1,128)} %bitcast.1), calls=%async_computation | async-start | bytes 786432 | tf_op jit(solution)/shard_map/all_to_all | solution.py:210
  24.1 0.0 copy-start.3
  24.1 0.0 copy-done
  24.2 0.0 copy-done.1
  24.2 0.0 copy-done.2
  24.2 0.6 %copy-done.3 = f32[256]{0:T(256)S(1)} copy-done((f32[256]{0:T(256)S(1)}, f32[256]{0:T(256)}, u32[]{:S(2)}) %copy-start.3) | copy-done | bytes 1048
  24.8 1.8 %local_grads.1 = (f32[512,256]{1,0:T(8,128)S(1)}, f32[512,256]{1,0:T(8,128)S(1)}, f32[512,256]{1,0:T(8,128)S(1)}, f32[8,128]{1,0:T(8,128)S(1)}) custom-call(f32[1,256]{1,0:T(1,128)S(1)} %bitcast.14, f32[512,128]{1,0:T(8,128)S(1)} %get-tuple-element.16.cos_ref, f32[512,128]{1,0:T(8,128)S(1)} %get-tuple-element.17.sin_ref, bf16[1,512,256]{2,1,0:T(8,128)(2,1)S(1)} %copy-done.2, ...), custom_call_target="tpu_custom_call" | custom-call | tf_op jit(solution)/shard_map/local_grads/pallas_call | solution.py:254
  26.6 6.1 %all-to-all-done = f32[64,1,1536]{2,1,0:T(1,128)S(1)} async-done(((f32[64,1,1536]{2,1,0:T(1,128)}), f32[64,1,1536]{2,1,0:T(1,128)S(1)}, u32[]{:S(2)}, u32[]{:S(2)}) %all-to-all-start) | async-done | bytes 393248 | tf_op jit(solution)/shard_map/all_to_all | solution.py:210
  32.7 0.2 scan.1
  32.9 19.0 %all_to_all.15 = f32[64,1,1280]{2,1,0:T(1,128)S(1)} all-to-all(f32[64,1,1280]{2,1,0:T(1,128)S(1)} %bitcast.11), channel_id=1, replica_groups={{36,37,38,39,32,33,34,35,44,45,46,47,40,41,42,43,52,53,54,55,48,49,50,5..., dimensions={0} | all-to-all | bytes 655360 | tf_op jit(solution)/shard_map/all_to_all | solution.py:210
  51.9 9.2 %all_to_all.16 = f32[8,1,256]{2,1,0:T(1,128)S(1)} all-to-all(f32[8,1,256]{2,1,0:T(1,128)S(1)} %bitcast.13), channel_id=1, replica_groups={{256,320,384,448,0,64,128,192},{257,321,385,449,1,65,129,193},{258,322,..., dimensions={0} | all-to-all | bytes 16384 | tf_op jit(solution)/shard_map/all_to_all | solution.py:210
  61.0 1.4 %final.1 = (bf16[1,512,256]{2,1,0:T(8,128)(2,1)}, bf16[1,512,256]{2,1,0:T(8,128)(2,1)}, bf16[1,512,256]{2,1,0:T(8,128)(2,1)}, f32[1,256]{1,0:T(1,128)}) custom-call(f32[1,256]{1,0:T(1,128)S(1)} %bitcast.16, f32[512,128]{1,0:T(8,128)S(1)} %get-tuple-element.16.cos_ref, f32[512,128]{1,0:T(8,128)S(1)} %get-tuple-element.17.sin_ref, ...), custom_call_target="tpu_custom_call" | custom-call | tf_op jit(solution)/shard_map/final/pallas_call | solution.py:284
  (1 shorter events, 0.0 us)
Async XLA Ops:
  3.8 20.3 %copy-start = (bf16[1,512,256]{2,1,0:T(8,128)(2,1)S(1)}, bf16[1,512,256]{2,1,0:T(8,128)(2,1)}, u32[]{:S(2)}) copy-start(bf16[1,512,256]{2,1,0:T(8,128)(2,1)} %v_ref.3) | copy-start | bytes 786436
  3.8 20.3 %copy-start.1 = (bf16[1,512,256]{2,1,0:T(8,128)(2,1)S(1)}, bf16[1,512,256]{2,1,0:T(8,128)(2,1)}, u32[]{:S(2)}) copy-start(bf16[1,512,256]{2,1,0:T(8,128)(2,1)} %g_ref.3) | copy-start | bytes 786436
  3.8 20.3 %copy-start.2 = (bf16[1,512,256]{2,1,0:T(8,128)(2,1)S(1)}, bf16[1,512,256]{2,1,0:T(8,128)(2,1)}, u32[]{:S(2)}) copy-start(bf16[1,512,256]{2,1,0:T(8,128)(2,1)} %q_ref.1) | copy-start | bytes 786436
  3.9 28.8 %all-to-all-start = ((f32[64,1,1536]{2,1,0:T(1,128)}), f32[64,1,1536]{2,1,0:T(1,128)S(1)}, u32[]{:S(2)}, u32[]{:S(2)}) async-start(f32[64,1,1536]{2,1,0:T(1,128)} %bitcast.1), calls=%async_computation | async-start | bytes 786432 | tf_op jit(solution)/shard_map/all_to_all | solution.py:210
  24.1 0.7 %copy-start.3 = (f32[256]{0:T(256)S(1)}, f32[256]{0:T(256)}, u32[]{:S(2)}) copy-start(f32[256]{0:T(256)} %param.12) | copy-start | bytes 3076

commit v5 on v4

--- a/solution.py
+++ b/solution.py
@@ -18,6 +18,7 @@
 TABLE_ROWS = 168
 SEND = 12
 BACK = 10
+CHUNKS = 2
 SIDE = 8
 FIRST = (4, 4)
 FIRST_DP = 4
@@ -170,9 +171,15 @@
 
 def final_kernel(
     scale, factor, gain_ref, cos_ref, sin_ref, krot_ref, v_ref, g_ref, dq_ref, dk_ref, dv_ref, recv_ref, parts_ref,
-    gq_ref, gk_ref, gv_ref, total_ref,
+    gq_hbm, gk_hbm, gv_hbm, total_hbm, gq_ref, gk_ref, gv_ref, total_ref, sems,
 ):
-    cosine, sine = cos_ref[...], sin_ref[...]
+    copies = []
+
+    def write(source, target):
+        copies.append(pltpu.make_async_copy(source, target, sems.at[len(copies)]))
+        copies[-1].start()
+
+    states, backs = [], []
     for head in range(HEADS):
         lanes = slice(head * DIM, (head + 1) * DIM)
         parts = parts_ref[pl.ds(head, parts_ref.shape[0] // HEADS, stride=HEADS), :]
@@ -180,17 +187,39 @@
 
         def matrix(first):
             halves = [recv_ref[pl.ds(first + half, HALF, stride=BACK), :] for half in range(2)]
-            return jnp.concatenate(halves, axis=0).astype(jnp.bfloat16)
-
-        state = matrix(2 * head)
-        back = matrix(4 + 2 * head)
-        dq = scale * dot(g_ref[0, :, lanes], state, 1, 0)
-        dq = dq_ref[:, lanes] + (dq * cosine - swap(dq) * sine)
-        gq_ref[0, :, lanes] = (dq * gain_ref[:, lanes]).astype(jnp.bfloat16)
-        dk = scale * dot(v_ref[0, :, lanes], back, 1, 0)
-        gk_ref[0, :, lanes] = (dk_ref[:, lanes] + (dk * cosine - swap(dk) * sine)).astype(jnp.bfloat16)
-        dv = scale * dot(krot_ref[:, lanes], back, 1, 1)
-        gv_ref[0, :, lanes] = (dv_ref[:, lanes] + dv).astype(jnp.bfloat16)
+            return scale * jnp.concatenate(halves, axis=0)
+
+        states.append(matrix(2 * head))
+        backs.append(matrix(4 + 2 * head))
+    write(total_ref, total_hbm)
+
+    def both(x):
+        return jnp.concatenate([x, swap(x)], axis=1).astype(jnp.bfloat16)
+
+    def unrotate(products, rows):
+        return products[:, :DIM] * cos_ref[rows, :] - products[:, DIM:] * sin_ref[rows, :]
+
+    states = [both(x) for x in states]
+    backs = [both(x) for x in backs]
+    for start in range(0, ROWS, ROWS // CHUNKS):
+        rows = slice(start, start + ROWS // CHUNKS)
+        for head in range(HEADS):
+            lanes = slice(head * DIM, (head + 1) * DIM)
+            dv = dot(krot_ref[rows, lanes], backs[head][:, :DIM], 1, 1)
+            gv_ref[0, rows, lanes] = (dv_ref[rows, lanes] + dv).astype(jnp.bfloat16)
+        write(gv_ref.at[:, rows], gv_hbm.at[:, rows])
+        for head in range(HEADS):
+            lanes = slice(head * DIM, (head + 1) * DIM)
+            dq = dq_ref[rows, lanes] + unrotate(dot(g_ref[0, rows, lanes], states[head], 1, 0), rows)
+            gq_ref[0, rows, lanes] = (dq * gain_ref[:, lanes]).astype(jnp.bfloat16)
+        write(gq_ref.at[:, rows], gq_hbm.at[:, rows])
+        for head in range(HEADS):
+            lanes = slice(head * DIM, (head + 1) * DIM)
+            dk = dk_ref[rows, lanes] + unrotate(dot(v_ref[0, rows, lanes], backs[head], 1, 0), rows)
+            gk_ref[0, rows, lanes] = dk.astype(jnp.bfloat16)
+        write(gk_ref.at[:, rows], gk_hbm.at[:, rows])
+    for copy in copies:
+        copy.wait()
 
 
 VMEM = pl.BlockSpec(memory_space=pltpu.VMEM)
@@ -285,7 +314,14 @@
         functools.partial(final_kernel, scale, factor),
         out_shape=(shape(*tokens, dtype=jnp.bfloat16),) * 3 + (shape(1, width),),
         in_specs=[VMEM] * 11,
-        out_specs=(VMEM,) * 4,
+        out_specs=(HBM,) * 4,
+        scratch_shapes=[
+            pltpu.VMEM(tokens, jnp.bfloat16),
+            pltpu.VMEM(tokens, jnp.bfloat16),
+            pltpu.VMEM(tokens, jnp.bfloat16),
+            pltpu.VMEM((1, width), jnp.float32),
+            pltpu.SemaphoreType.DMA((1 + 3 * CHUNKS,)),
+        ],
         compiler_params=PARAMS,
         name="final",
     )(gain_row, cosine, sine, krot, values, out_grad, dq, dk, dv, states, gain_parts)

time: 62.7 us -> 62.6 us (level)
  no operation moved by 1% of the time
where the time goes in v5:
time: 62.6 us; the launch traced here: 62.3 us
  blocking collectives  28.1 us (45%)
  starting transfers between devices  20.3 us (32%)
  waiting for transfers between devices  6.09 us (10%)
  Pallas kernels  5.8 us (9%)
  between operations  1.36 us (2%)
  local copies, waits for them, and re-layouts  0.66 us (1%)
    all_to_all x2, blocking collectives, exchange(): lax.all_to_all(pieces, axis, 0, 0, axis_index_groups=groups, tiled=True)  28.1 us
    all_to_all x1, starting transfers between devices, exchange(): lax.all_to_all(pieces, axis, 0, 0, axis_index_groups=groups, tiled=True)  20.3 us
    all_to_all x1, waiting for transfers between devices, exchange(): lax.all_to_all(pieces, axis, 0, 0, axis_index_groups=groups, tiled=True)  6.09 us
    pallas_call x1, Pallas kernels, local(): pl.pallas_call(states_kernel, out_shape=(shape(shards * SEND, DIM), shape...  2.53 us
    pallas_call x1, Pallas kernels, local(): pl.pallas_call(functools.partial(local_kernel, scale), out_shape=(shape(r...  1.78 us
    pallas_call x1, Pallas kernels, local(): pl.pallas_call(functools.partial(final_kernel, scale, factor), out_shape=...  1.26 us
  transfers between devices with their start and end apart: 1, of which 1 were waited for; matrix products, arithmetic and copies ran while one was open for 0% of the time, Pallas kernels for 3%

profile of v5, /device:TPU:1, one launch (start us, length us, event | category | flops | bytes accessed | tf_op | source)
XLA Modules:
  0.0 62.3 jit_solution(8498772084822982807)
XLA Ops:
  1.3 2.5 %states.1 = (f32[768,128]{1,0:T(8,128)}, bf16[512,256]{1,0:T(8,128)(2,1)S(1)}, f32[512,128]{1,0:T(8,128)S(1)}, f32[512,128]{1,0:T(8,128)S(1)}) custom-call(s32[1,1]{1,0:T(1,128)S(6)} %copy.15.off_ref, f32[168,128]{1,0:T(8,128)} %constant.4.clone.ctab_hbm, f32[168,128]{1,0:T(8,128)} %constant.5.clone.stab_hbm, bf16[1,512,256]{2,1,0:T(8,128)(2,1)} %q_ref.1, ...), custom_call_target="tpu_custom_call" | custom-call | tf_op jit(solution)/shard_map/states/pallas_call | solution.py:252
  3.8 0.0 copy-start
  3.8 0.0 copy-start.1
  3.8 0.0 copy-start.2
  3.9 20.3 %all-to-all-start = ((f32[64,1,1536]{2,1,0:T(1,128)}), f32[64,1,1536]{2,1,0:T(1,128)S(1)}, u32[]{:S(2)}, u32[]{:S(2)}) async-start(f32[64,1,1536]{2,1,0:T(1,128)} %bitcast.1), calls=%async_computation | async-start | bytes 786432 | tf_op jit(solution)/shard_map/all_to_all | solution.py:239
  24.1 0.0 copy-start.3
  24.1 0.0 copy-done
  24.2 0.0 copy-done.1
  24.2 0.0 copy-done.2
  24.2 0.6 %copy-done.3 = f32[256]{0:T(256)S(1)} copy-done((f32[256]{0:T(256)S(1)}, f32[256]{0:T(256)}, u32[]{:S(2)}) %copy-start.3) | copy-done | bytes 1048
  24.8 1.8 %local_grads.1 = (f32[512,256]{1,0:T(8,128)S(1)}, f32[512,256]{1,0:T(8,128)S(1)}, f32[512,256]{1,0:T(8,128)S(1)}, f32[8,128]{1,0:T(8,128)S(1)}) custom-call(f32[1,256]{1,0:T(1,128)S(1)} %bitcast.14, f32[512,128]{1,0:T(8,128)S(1)} %get-tuple-element.16.cos_ref, f32[512,128]{1,0:T(8,128)S(1)} %get-tuple-element.17.sin_ref, bf16[1,512,256]{2,1,0:T(8,128)(2,1)S(1)} %copy-done.2, ...), custom_call_target="tpu_custom_call" | custom-call | tf_op jit(solution)/shard_map/local_grads/pallas_call | solution.py:283
  26.6 6.1 %all-to-all-done = f32[64,1,1536]{2,1,0:T(1,128)S(1)} async-done(((f32[64,1,1536]{2,1,0:T(1,128)}), f32[64,1,1536]{2,1,0:T(1,128)S(1)}, u32[]{:S(2)}, u32[]{:S(2)}) %all-to-all-start) | async-done | bytes 393248 | tf_op jit(solution)/shard_map/all_to_all | solution.py:239
  32.7 0.2 scan.1
  32.9 19.0 %all_to_all.15 = f32[64,1,1280]{2,1,0:T(1,128)S(1)} all-to-all(f32[64,1,1280]{2,1,0:T(1,128)S(1)} %bitcast.11), channel_id=1, replica_groups={{36,37,38,39,32,33,34,35,44,45,46,47,40,41,42,43,52,53,54,55,48,49,50,5..., dimensions={0} | all-to-all | bytes 655360 | tf_op jit(solution)/shard_map/all_to_all | solution.py:239
  51.9 9.2 %all_to_all.16 = f32[8,1,256]{2,1,0:T(1,128)S(1)} all-to-all(f32[8,1,256]{2,1,0:T(1,128)S(1)} %bitcast.13), channel_id=1, replica_groups={{256,320,384,448,0,64,128,192},{257,321,385,449,1,65,129,193},{258,322,..., dimensions={0} | all-to-all | bytes 16384 | tf_op jit(solution)/shard_map/all_to_all | solution.py:239
  61.0 1.3 %final.1 = (bf16[1,512,256]{2,1,0:T(8,128)(2,1)}, bf16[1,512,256]{2,1,0:T(8,128)(2,1)}, bf16[1,512,256]{2,1,0:T(8,128)(2,1)}, f32[1,256]{1,0:T(1,128)}) custom-call(f32[1,256]{1,0:T(1,128)S(1)} %bitcast.16, f32[512,128]{1,0:T(8,128)S(1)} %get-tuple-element.16.cos_ref, f32[512,128]{1,0:T(8,128)S(1)} %get-tuple-element.17.sin_ref, ...), custom_call_target="tpu_custom_call" | custom-call | tf_op jit(solution)/shard_map/final/pallas_call | solution.py:313
  (1 shorter events, 0.0 us)
Async XLA Ops:
  3.8 20.3 %copy-start = (bf16[1,512,256]{2,1,0:T(8,128)(2,1)S(1)}, bf16[1,512,256]{2,1,0:T(8,128)(2,1)}, u32[]{:S(2)}) copy-start(bf16[1,512,256]{2,1,0:T(8,128)(2,1)} %v_ref.3) | copy-start | bytes 786436
  3.8 20.3 %copy-start.1 = (bf16[1,512,256]{2,1,0:T(8,128)(2,1)S(1)}, bf16[1,512,256]{2,1,0:T(8,128)(2,1)}, u32[]{:S(2)}) copy-start(bf16[1,512,256]{2,1,0:T(8,128)(2,1)} %g_ref.3) | copy-start | bytes 786436
  3.8 20.3 %copy-start.2 = (bf16[1,512,256]{2,1,0:T(8,128)(2,1)S(1)}, bf16[1,512,256]{2,1,0:T(8,128)(2,1)}, u32[]{:S(2)}) copy-start(bf16[1,512,256]{2,1,0:T(8,128)(2,1)} %q_ref.1) | copy-start | bytes 786436
  3.9 28.8 %all-to-all-start = ((f32[64,1,1536]{2,1,0:T(1,128)}), f32[64,1,1536]{2,1,0:T(1,128)S(1)}, u32[]{:S(2)}, u32[]{:S(2)}) async-start(f32[64,1,1536]{2,1,0:T(1,128)} %bitcast.1), calls=%async_computation | async-start | bytes 786432 | tf_op jit(solution)/shard_map/all_to_all | solution.py:239
  24.1 0.7 %copy-start.3 = (f32[256]{0:T(256)S(1)}, f32[256]{0:T(256)}, u32[]{:S(2)}) copy-start(f32[256]{0:T(256)} %param.12) | copy-start | bytes 3076

commit v6 on v5

--- a/solution.py
+++ b/solution.py
@@ -44,9 +44,14 @@
     return pltpu.roll(x, HALF, 1)
 
 
+def local_here(early):
+    return (lax.rem(lax.axis_index("dp"), 2) == 0) == early
+
+
 def states_kernel(
-    off_ref, ctab_hbm, stab_hbm, q_hbm, k_hbm, v_hbm, g_hbm, send_ref, krot_ref, cos_ref, sin_ref,
-    ctab_ref, stab_ref, q_ref, k_ref, v_ref, g_ref, sems,
+    scale, off_ref, ctab_hbm, stab_hbm, q_hbm, k_hbm, v_hbm, g_hbm, gain_hbm,
+    send_ref, krot_ref, cos_ref, sin_ref, dq_ref, dk_ref, dv_ref, part_ref,
+    ctab_ref, stab_ref, q_ref, k_ref, v_ref, g_ref, gain_ref, sems,
 ):
     pairs = (
         (ctab_hbm, ctab_ref),
@@ -55,6 +60,7 @@
         (v_hbm, v_ref),
         (q_hbm, q_ref),
         (g_hbm, g_ref),
+        (gain_hbm, gain_ref),
     )
     copies = [pltpu.make_async_copy(src, dst, sems.at[i]) for i, (src, dst) in enumerate(pairs)]
     for copy in copies:
@@ -100,8 +106,14 @@
             send_ref[pl.ds(4 + at, HALF, stride=SEND), :] = gq[rows, :DIM]
             send_ref[pl.ds(8 + at, HALF, stride=SEND), :] = gq[rows, DIM:]
 
-
-def local_kernel(
+    @pl.when(local_here(True))
+    def _():
+        local_grads(
+            scale, gain_ref, cos_ref, sin_ref, q_ref, krot_ref, v_ref, g_ref, dq_ref, dk_ref, dv_ref, part_ref
+        )
+
+
+def local_grads(
     scale, gain_ref, cos_ref, sin_ref, q_ref, krot_ref, v_ref, g_ref, dq_ref, dk_ref, dv_ref, part_ref
 ):
     cosine, sine = cos_ref[...], sin_ref[...]
@@ -126,6 +138,24 @@
         dq = dq * cosine - swap(dq) * sine
         dq_ref[:, lanes] = dq
         part_ref[head : head + 1, :] = jnp.sum(dq * q, axis=0, keepdims=True)
+
+
+def local_kernel(
+    scale, gain_ref, cos_ref, sin_ref, q_ref, krot_ref, v_ref, g_ref, dq_in, dk_in, dv_in, part_in,
+    dq_ref, dk_ref, dv_ref, part_ref,
+):
+    @pl.when(local_here(False))
+    def _():
+        local_grads(
+            scale, gain_ref, cos_ref, sin_ref, q_ref, krot_ref, v_ref, g_ref, dq_ref, dk_ref, dv_ref, part_ref
+        )
+
+    @pl.when(local_here(True))
+    def _():
+        dq_ref[...] = dq_in[...]
+        dk_ref[...] = dk_in[...]
+        dv_ref[...] = dv_in[...]
+        part_ref[...] = part_in[...]
 
 
 def rank(shard):
@@ -249,16 +279,18 @@
     order = sorted(range(shards), key=rank)
     tokens = queries.shape
 
-    sent, krot, cosine, sine = pl.pallas_call(
-        states_kernel,
+    local_shapes = (shape(rows, width),) * 3 + (shape(8, DIM),)
+    sent, krot, cosine, sine, *early = pl.pallas_call(
+        functools.partial(states_kernel, scale),
         out_shape=(
             shape(shards * SEND, DIM),
             shape(rows, width, dtype=jnp.bfloat16),
             shape(rows, DIM),
             shape(rows, DIM),
+            *local_shapes,
         ),
-        in_specs=[SMEM] + [HBM] * 6,
-        out_specs=(VMEM,) * 4,
+        in_specs=[SMEM] + [HBM] * 7,
+        out_specs=(VMEM,) * 8,
         scratch_shapes=[
             pltpu.VMEM(cos_table.shape, jnp.float32),
             pltpu.VMEM(cos_table.shape, jnp.float32),
@@ -266,7 +298,8 @@
             pltpu.VMEM(tokens, jnp.bfloat16),
             pltpu.VMEM(tokens, jnp.bfloat16),
             pltpu.VMEM(tokens, jnp.bfloat16),
-            pltpu.SemaphoreType.DMA((6,)),
+            pltpu.VMEM((1, width), jnp.float32),
+            pltpu.SemaphoreType.DMA((7,)),
         ],
         compiler_params=PARAMS,
         name="states",
@@ -274,20 +307,23 @@
         offsets,
         *(
             pltpu.with_memory_space_constraint(x, pltpu.HBM)
-            for x in (jnp.asarray(cos_table), jnp.asarray(sin_table), queries, keys, values, out_grad)
-        )
+            for x in (
+                jnp.asarray(cos_table), jnp.asarray(sin_table), queries, keys, values, out_grad, gain_row
+            )
+        ),
     )
 
     received = exchange(sent, "ctx", order)
 
     dq, dk, dv, part = pl.pallas_call(
         functools.partial(local_kernel, scale),
-        out_shape=(shape(rows, width), shape(rows, width), shape(rows, width), shape(8, DIM)),
-        in_specs=[VMEM] * 7,
+        out_shape=local_shapes,
+        in_specs=[VMEM] * 11,
         out_specs=(VMEM,) * 4,
+        input_output_aliases={7: 0, 8: 1, 9: 2, 10: 3},
         compiler_params=PARAMS,
         name="local_grads",
-    )(gain_row, cosine, sine, queries, krot, values, out_grad)
+    )(gain_row, cosine, sine, queries, krot, values, out_grad, *early)
 
     scanned = pl.pallas_call(
         functools.partial(scan_kernel, scale, shards),

time: 62.6 us -> 61.4 us (0.981)
  waiting for transfers between devices: 6.09 us -> 4.43 us
  Pallas kernels: 5.8 us -> 5.07 us
  local copies, waits for them, and re-layouts: 0.66 us -> 1.38 us
    all_to_all x1, waiting for transfers between devices: 6.09 us -> 4.43 us  [exchange(): lax.all_to_all(pieces, axis, 0, 0, axis_index_groups=groups, tiled=True)]
    pallas_call x2, Pallas kernels: 4.31 us -> 3.59 us  [the longest x1 1.8 us: local(): pl.pallas_call(functools.partial(states_kernel, scale), out_shape=(shape(...]
    unnamed x8 -> x10, local copies, waits for them, and re-layouts: 0.66 us -> 1.38 us
where the time goes in v6:
time: 61.4 us; the launch traced here: 61.1 us
  blocking collectives  28.6 us (47%)
  starting transfers between devices  20.3 us (33%)
  Pallas kernels  5.07 us (8%)
  waiting for transfers between devices  4.43 us (7%)
  local copies, waits for them, and re-layouts  1.38 us (2%)
  between operations  1.35 us (2%)
    all_to_all x2, blocking collectives, exchange(): lax.all_to_all(pieces, axis, 0, 0, axis_index_groups=groups, tiled=True)  28.6 us
    all_to_all x1, starting transfers between devices, exchange(): lax.all_to_all(pieces, axis, 0, 0, axis_index_groups=groups, tiled=True)  20.3 us
    all_to_all x1, waiting for transfers between devices, exchange(): lax.all_to_all(pieces, axis, 0, 0, axis_index_groups=groups, tiled=True)  4.43 us
    pallas_call x1, Pallas kernels, local(): pl.pallas_call(functools.partial(states_kernel, scale), out_shape=(shape(...  1.8 us
    pallas_call x1, Pallas kernels, local(): pl.pallas_call(functools.partial(local_kernel, scale), out_shape=local_sh...  1.78 us
    unnamed x10, local copies, waits for them, and re-layouts  1.38 us
    pallas_call x1, Pallas kernels, local(): pl.pallas_call(functools.partial(final_kernel, scale, factor), out_shape=...  1.26 us
  transfers between devices with their start and end apart: 1, of which 1 were waited for; matrix products, arithmetic and copies ran while one was open for 0% of the time, Pallas kernels for 3%

profile of v6, /device:TPU:1, one launch (start us, length us, event | category | flops | bytes accessed | tf_op | source)
XLA Modules:
  0.0 61.1 jit_solution(11540871654670546729)
XLA Ops:
  1.3 1.8 %states.1 = (f32[768,128]{1,0:T(8,128)S(1)}, bf16[512,256]{1,0:T(8,128)(2,1)S(1)}, f32[512,128]{1,0:T(8,128)S(1)}, f32[512,128]{1,0:T(8,128)S(1)}, f32[512,256]{...) custom-call(s32[1,1]{1,0:T(1,128)S(6)} %copy.23.off_ref, ...), custom_call_target="tpu_custom_call" | custom-call | tf_op jit(solution)/shard_map/states/pallas_call | solution.py:283
  3.1 0.0 copy-start.3
  3.1 0.7 %copy-done.3 = f32[768,128]{1,0:T(8,128)} copy-done((f32[768,128]{1,0:T(8,128)}, f32[768,128]{1,0:T(8,128)S(1)}, u32[]{:S(2)}) %copy-start.3) | copy-done | bytes 393240
  3.8 0.0 copy-start
  3.8 0.0 copy-start.1
  3.8 0.0 copy-start.2
  3.8 20.3 %all-to-all-start = ((f32[64,1,1536]{2,1,0:T(1,128)}), f32[64,1,1536]{2,1,0:T(1,128)S(1)}, u32[]{:S(2)}, u32[]{:S(2)}) async-start(f32[64,1,1536]{2,1,0:T(1,128)} %bitcast.12), calls=%async_computation | async-start | bytes 786432 | tf_op jit(solution)/shard_map/all_to_all | solution.py:269
  24.1 0.0 copy-start.4
  24.1 0.0 copy-done
  24.1 0.0 copy-done.1
  24.1 0.0 copy-done.2
  24.1 0.6 %copy-done.4 = f32[256]{0:T(256)S(1)} copy-done((f32[256]{0:T(256)S(1)}, f32[256]{0:T(256)}, u32[]{:S(2)}) %copy-start.4) | copy-done | bytes 1048
  24.8 1.8 %local_grads.1 = (f32[512,256]{1,0:T(8,128)S(1)}, f32[512,256]{1,0:T(8,128)S(1)}, f32[512,256]{1,0:T(8,128)S(1)}, f32[8,128]{1,0:T(8,128)S(1)}) custom-call(f32[1,256]{1,0:T(1,128)S(1)} %bitcast.16, f32[512,128]{1,0:T(8,128)S(1)} %get-tuple-element.20.cos_ref, ...), custom_call_target="tpu_custom_call", output_to_operand_aliasing={{0}: (7, {}), {1}: (8, {}), {2}: (9, {}), {3}: (10, {})} | custom-call | tf_op jit(solution)/shard_map/local_grads/pallas_call | solution.py:318
  26.6 4.4 %all-to-all-done = f32[64,1,1536]{2,1,0:T(1,128)S(1)} async-done(((f32[64,1,1536]{2,1,0:T(1,128)}), f32[64,1,1536]{2,1,0:T(1,128)S(1)}, u32[]{:S(2)}, u32[]{:S(2)}) %all-to-all-start) | async-done | bytes 393248 | tf_op jit(solution)/shard_map/all_to_all | solution.py:269
  31.0 0.2 scan.1
  31.2 17.3 %all_to_all.15 = f32[64,1,1280]{2,1,0:T(1,128)S(1)} all-to-all(f32[64,1,1280]{2,1,0:T(1,128)S(1)} %bitcast.11), channel_id=1, replica_groups={{36,37,38,39,32,33,34,35,44,45,46,47,40,41,42,43,52,53,54,55,48,49,50,5..., dimensions={0} | all-to-all | bytes 655360 | tf_op jit(solution)/shard_map/all_to_all | solution.py:269
  48.5 11.3 %all_to_all.16 = f32[8,1,256]{2,1,0:T(1,128)S(1)} all-to-all(f32[8,1,256]{2,1,0:T(1,128)S(1)} %bitcast.14), channel_id=1, replica_groups={{256,320,384,448,0,64,128,192},{257,321,385,449,1,65,129,193},{258,322,..., dimensions={0} | all-to-all | bytes 16384 | tf_op jit(solution)/shard_map/all_to_all | solution.py:269
  59.9 1.3 %final.1 = (bf16[1,512,256]{2,1,0:T(8,128)(2,1)}, bf16[1,512,256]{2,1,0:T(8,128)(2,1)}, bf16[1,512,256]{2,1,0:T(8,128)(2,1)}, f32[1,256]{1,0:T(1,128)}) custom-call(f32[1,256]{1,0:T(1,128)S(1)} %bitcast.18, f32[512,128]{1,0:T(8,128)S(1)} %get-tuple-element.20.cos_ref, f32[512,128]{1,0:T(8,128)S(1)} %get-tuple-element.21.sin_ref, ...), custom_call_target="tpu_custom_call" | custom-call | tf_op jit(solution)/shard_map/final/pallas_call | solution.py:349
  (1 shorter events, 0.0 us)
Async XLA Ops:
  3.1 0.7 %copy-start.3 = (f32[768,128]{1,0:T(8,128)}, f32[768,128]{1,0:T(8,128)S(1)}, u32[]{:S(2)}) copy-start(f32[768,128]{1,0:T(8,128)S(1)} %get-tuple-element.30) | copy-start | bytes 1179652
  3.8 20.3 %copy-start = (bf16[1,512,256]{2,1,0:T(8,128)(2,1)S(1)}, bf16[1,512,256]{2,1,0:T(8,128)(2,1)}, u32[]{:S(2)}) copy-start(bf16[1,512,256]{2,1,0:T(8,128)(2,1)} %v_ref.3) | copy-start | bytes 786436
  3.8 20.3 %copy-start.1 = (bf16[1,512,256]{2,1,0:T(8,128)(2,1)S(1)}, bf16[1,512,256]{2,1,0:T(8,128)(2,1)}, u32[]{:S(2)}) copy-start(bf16[1,512,256]{2,1,0:T(8,128)(2,1)} %g_ref.3) | copy-start | bytes 786436
  3.8 20.3 %copy-start.2 = (bf16[1,512,256]{2,1,0:T(8,128)(2,1)S(1)}, bf16[1,512,256]{2,1,0:T(8,128)(2,1)}, u32[]{:S(2)}) copy-start(bf16[1,512,256]{2,1,0:T(8,128)(2,1)} %q_ref.1) | copy-start | bytes 786436
  3.8 27.2 %all-to-all-start = ((f32[64,1,1536]{2,1,0:T(1,128)}), f32[64,1,1536]{2,1,0:T(1,128)S(1)}, u32[]{:S(2)}, u32[]{:S(2)}) async-start(f32[64,1,1536]{2,1,0:T(1,128)} %bitcast.12), calls=%async_computation | async-start | bytes 786432 | tf_op jit(solution)/shard_map/all_to_all | solution.py:269
  24.1 0.7 %copy-start.4 = (f32[256]{0:T(256)S(1)}, f32[256]{0:T(256)}, u32[]{:S(2)}) copy-start(f32[256]{0:T(256)} %param.12) | copy-start | bytes 3076

commit v7 on v6

--- a/solution.py
+++ b/solution.py
@@ -21,7 +21,7 @@
 CHUNKS = 2
 SIDE = 8
 FIRST = (4, 4)
-FIRST_DP = 4
+FIRST_DP = 5
 
 
 def rotary_tables():
@@ -199,9 +199,9 @@
             out_ref[HEADS * copy + head : HEADS * copy + head + 1, :] = part
 
 
-def final_kernel(
-    scale, factor, gain_ref, cos_ref, sin_ref, krot_ref, v_ref, g_ref, dq_ref, dk_ref, dv_ref, recv_ref, parts_ref,
-    gq_hbm, gk_hbm, gv_hbm, total_hbm, gq_ref, gk_ref, gv_ref, total_ref, sems,
+def write_grads(
+    scale, gain_ref, cos_ref, sin_ref, krot_ref, v_ref, g_ref, dq_ref, dk_ref, dv_ref, recv_ref,
+    gq_hbm, gk_hbm, gv_hbm, gq_ref, gk_ref, gv_ref, sems,
 ):
     copies = []
 
@@ -209,19 +209,9 @@
         copies.append(pltpu.make_async_copy(source, target, sems.at[len(copies)]))
         copies[-1].start()
 
-    states, backs = [], []
-    for head in range(HEADS):
-        lanes = slice(head * DIM, (head + 1) * DIM)
-        parts = parts_ref[pl.ds(head, parts_ref.shape[0] // HEADS, stride=HEADS), :]
-        total_ref[:, lanes] = jnp.sum(parts, axis=0, keepdims=True) * factor
-
-        def matrix(first):
-            halves = [recv_ref[pl.ds(first + half, HALF, stride=BACK), :] for half in range(2)]
-            return scale * jnp.concatenate(halves, axis=0)
-
-        states.append(matrix(2 * head))
-        backs.append(matrix(4 + 2 * head))
-    write(total_ref, total_hbm)
+    def matrix(first):
+        halves = [recv_ref[pl.ds(first + half, HALF, stride=BACK), :] for half in range(2)]
+        return scale * jnp.concatenate(halves, axis=0)
 
     def both(x):
         return jnp.concatenate([x, swap(x)], axis=1).astype(jnp.bfloat16)
@@ -229,8 +219,8 @@
     def unrotate(products, rows):
         return products[:, :DIM] * cos_ref[rows, :] - products[:, DIM:] * sin_ref[rows, :]
 
-    states = [both(x) for x in states]
-    backs = [both(x) for x in backs]
+    states = [both(matrix(2 * head)) for head in range(HEADS)]
+    backs = [both(matrix(4 + 2 * head)) for head in range(HEADS)]
     for start in range(0, ROWS, ROWS // CHUNKS):
         rows = slice(start, start + ROWS // CHUNKS)
         for head in range(HEADS):
@@ -250,6 +240,29 @@
         write(gk_ref.at[:, rows], gk_hbm.at[:, rows])
     for copy in copies:
         copy.wait()
+
+
+def waiting_kernel(scale, *refs):
+    @pl.when(local_here(False))
+    def _():
+        write_grads(scale, *refs)
+
+
+def final_kernel(scale, factor, *refs):
+    operands, parts_ref, grads, total_hbm = refs[:10], refs[10], refs[14:17], refs[17]
+    *scratch, sems, total_ref, total_sem = refs[18:]
+    for head in range(HEADS):
+        lanes = slice(head * DIM, (head + 1) * DIM)
+        parts = parts_ref[pl.ds(head, parts_ref.shape[0] // HEADS, stride=HEADS), :]
+        total_ref[:, lanes] = jnp.sum(parts, axis=0, keepdims=True) * factor
+    copy = pltpu.make_async_copy(total_ref, total_hbm, total_sem)
+    copy.start()
+
+    @pl.when(local_here(True))
+    def _():
+        write_grads(scale, *operands, *grads, *scratch, sems)
+
+    copy.wait()
 
 
 VMEM = pl.BlockSpec(memory_space=pltpu.VMEM)
@@ -344,23 +357,33 @@
         compiler_params=PARAMS,
         name="gain_part",
     )(states)
+
+    operands = (gain_row, cosine, sine, krot, values, out_grad, dq, dk, dv, states)
+    grad_shapes = (shape(*tokens, dtype=jnp.bfloat16),) * 3
+    scratch = [pltpu.VMEM(tokens, jnp.bfloat16)] * 3 + [pltpu.SemaphoreType.DMA((3 * CHUNKS,))]
+    grads = pl.pallas_call(
+        functools.partial(waiting_kernel, scale),
+        out_shape=grad_shapes,
+        in_specs=[VMEM] * 10,
+        out_specs=(HBM,) * 3,
+        scratch_shapes=scratch,
+        compiler_params=PARAMS,
+        name="final_core1",
+    )(*operands)
+
+    gain_part, grads = lax.optimization_barrier((gain_part, grads))
     gain_parts = exchange(gain_part, "dp", [(FIRST_DP + i) % groups for i in range(groups)])
 
     grad_queries, grad_keys, grad_values, grad_gain = pl.pallas_call(
         functools.partial(final_kernel, scale, factor),
-        out_shape=(shape(*tokens, dtype=jnp.bfloat16),) * 3 + (shape(1, width),),
-        in_specs=[VMEM] * 11,
+        out_shape=grad_shapes + (shape(1, width),),
+        in_specs=[VMEM] * 11 + [HBM] * 3,
         out_specs=(HBM,) * 4,
-        scratch_shapes=[
-            pltpu.VMEM(tokens, jnp.bfloat16),
-            pltpu.VMEM(tokens, jnp.bfloat16),
-            pltpu.VMEM(tokens, jnp.bfloat16),
-            pltpu.VMEM((1, width), jnp.float32),
-            pltpu.SemaphoreType.DMA((1 + 3 * CHUNKS,)),
-        ],
+        scratch_shapes=scratch + [pltpu.VMEM((1, width), jnp.float32), pltpu.SemaphoreType.DMA],
+        input_output_aliases={11: 0, 12: 1, 13: 2},
         compiler_params=PARAMS,
         name="final",
-    )(gain_row, cosine, sine, krot, values, out_grad, dq, dk, dv, states, gain_parts)
+    )(*operands, gain_parts, *grads)
     return grad_queries, grad_keys, grad_values, grad_gain.reshape(width)
 
 

time: 61.4 us -> 60.7 us (0.989)
  blocking collectives: 28.6 us -> 27.2 us
  Pallas kernels: 5.07 us -> 5.71 us
    all_to_all x2, blocking collectives: 28.6 us -> 27.2 us  [exchange(): lax.all_to_all(pieces, axis, 0, 0, axis_index_groups=groups, tiled=True)]
    pallas_call x0 -> x1, Pallas kernels: none -> 1.27 us  [local(): pl.pallas_call(functools.partial(waiting_kernel, scale), out_shape=grad_s...]
    pallas_call x1, Pallas kernels: 1.26 us -> 0.63 us  [local(): pl.pallas_call(functools.partial(final_kernel, scale, factor), out_shape=...]
where the time goes in v7:
time: 60.7 us; the launch traced here: 60.4 us
  blocking collectives  27.2 us (45%)
  starting transfers between devices  20.3 us (33%)
  Pallas kernels  5.71 us (9%)
  waiting for transfers between devices  4.43 us (7%)
  local copies, waits for them, and re-layouts  1.4 us (2%)
  between operations  1.36 us (2%)
    all_to_all x2, blocking collectives, exchange(): lax.all_to_all(pieces, axis, 0, 0, axis_index_groups=groups, tiled=True)  27.2 us
    all_to_all x1, starting transfers between devices, exchange(): lax.all_to_all(pieces, axis, 0, 0, axis_index_groups=groups, tiled=True)  20.3 us
    all_to_all x1, waiting for transfers between devices, exchange(): lax.all_to_all(pieces, axis, 0, 0, axis_index_groups=groups, tiled=True)  4.43 us
    pallas_call x1, Pallas kernels, local(): pl.pallas_call(functools.partial(states_kernel, scale), out_shape=(shape(...  1.8 us
    pallas_call x1, Pallas kernels, local(): pl.pallas_call(functools.partial(local_kernel, scale), out_shape=local_sh...  1.78 us
    unnamed x10, local copies, waits for them, and re-layouts  1.4 us
    pallas_call x1, Pallas kernels, local(): pl.pallas_call(functools.partial(waiting_kernel, scale), out_shape=grad_s...  1.27 us
  transfers between devices with their start and end apart: 1, of which 1 were waited for; matrix products, arithmetic and copies ran while one was open for 0% of the time, Pallas kernels for 3%

profile of v7, /device:TPU:1, one launch (start us, length us, event | category | flops | bytes accessed | tf_op | source)
XLA Modules:
  0.0 60.4 jit_solution(14272657554523847131)
XLA Ops:
  1.3 1.8 %states.1 = (f32[768,128]{1,0:T(8,128)S(1)}, bf16[512,256]{1,0:T(8,128)(2,1)S(1)}, f32[512,128]{1,0:T(8,128)S(1)}, f32[512,128]{1,0:T(8,128)S(1)}, f32[512,256]{...) custom-call(s32[1,1]{1,0:T(1,128)S(6)} %copy.29.off_ref, ...), custom_call_target="tpu_custom_call" | custom-call | tf_op jit(solution)/shard_map/states/pallas_call | solution.py:296
  3.1 0.0 copy-start.3
  3.1 0.7 %copy-done.3 = f32[768,128]{1,0:T(8,128)} copy-done((f32[768,128]{1,0:T(8,128)}, f32[768,128]{1,0:T(8,128)S(1)}, u32[]{:S(2)}) %copy-start.3) | copy-done | bytes 393240
  3.8 0.0 copy-start
  3.8 0.0 copy-start.1
  3.8 0.0 copy-start.2
  3.8 20.3 %all-to-all-start = ((f32[64,1,1536]{2,1,0:T(1,128)}), f32[64,1,1536]{2,1,0:T(1,128)S(1)}, u32[]{:S(2)}, u32[]{:S(2)}) async-start(f32[64,1,1536]{2,1,0:T(1,128)} %bitcast.13), calls=%async_computation | async-start | bytes 786432 | tf_op jit(solution)/shard_map/all_to_all | solution.py:282
  24.1 0.0 copy-start.4
  24.1 0.0 copy-done
  24.1 0.0 copy-done.1
  24.1 0.0 copy-done.2
  24.2 0.6 %copy-done.4 = f32[256]{0:T(256)S(1)} copy-done((f32[256]{0:T(256)S(1)}, f32[256]{0:T(256)}, u32[]{:S(2)}) %copy-start.4) | copy-done | bytes 1048
  24.8 1.8 %local_grads.1 = (f32[512,256]{1,0:T(8,128)S(1)}, f32[512,256]{1,0:T(8,128)S(1)}, f32[512,256]{1,0:T(8,128)S(1)}, f32[8,128]{1,0:T(8,128)S(1)}) custom-call(f32[1,256]{1,0:T(1,128)S(1)} %bitcast.17, f32[512,128]{1,0:T(8,128)S(1)} %get-tuple-element.27.cos_ref.refs_1_, ...), custom_call_target="tpu_custom_call", output_to_operand_aliasing={{0}: (7, {}), {1}: (8, {}), {2}: (9, {}), {3}: (10, {})} | custom-call | tf_op jit(solution)/shard_map/local_grads/pallas_call | solution.py:331
  26.6 4.4 %all-to-all-done = f32[64,1,1536]{2,1,0:T(1,128)S(1)} async-done(((f32[64,1,1536]{2,1,0:T(1,128)}), f32[64,1,1536]{2,1,0:T(1,128)S(1)}, u32[]{:S(2)}, u32[]{:S(2)}) %all-to-all-start) | async-done | bytes 393248 | tf_op jit(solution)/shard_map/all_to_all | solution.py:282
  31.0 0.2 scan.1
  31.2 17.3 %all_to_all.15 = f32[64,1,1280]{2,1,0:T(1,128)S(1)} all-to-all(f32[64,1,1280]{2,1,0:T(1,128)S(1)} %bitcast.12), channel_id=1, replica_groups={{36,37,38,39,32,33,34,35,44,45,46,47,40,41,42,43,52,53,54,55,48,49,50,5..., dimensions={0} | all-to-all | bytes 655360 | tf_op jit(solution)/shard_map/all_to_all | solution.py:282
  48.5 1.3 %final_core1.1 = (bf16[1,512,256]{2,1,0:T(8,128)(2,1)}, bf16[1,512,256]{2,1,0:T(8,128)(2,1)}, bf16[1,512,256]{2,1,0:T(8,128)(2,1)}) custom-call(f32[1,256]{1,0:T(1,128)S(1)} %bitcast.19, f32[512,128]{1,0:T(8,128)S(1)} %get-tuple-element.27.cos_ref.refs_1_, f32[512,128]{1,0:T(8,128)S(1)} %get-tuple-element.28.sin_ref.refs_2_, ...), custom_call_target="tpu_custom_call" | custom-call | tf_op jit(solution)/shard_map/final_core1/pallas_call | solution.py:364
  49.8 9.9 %all_to_all.16 = f32[8,1,256]{2,1,0:T(1,128)S(1)} all-to-all(f32[8,1,256]{2,1,0:T(1,128)S(1)} %bitcast.15), channel_id=1, replica_groups={{320,384,448,0,64,128,192,256},{321,385,449,1,65,129,193,257},{322,386,..., dimensions={0} | all-to-all | bytes 16384 | tf_op jit(solution)/shard_map/all_to_all | solution.py:282
  59.8 0.6 %final.1 = (bf16[1,512,256]{2,1,0:T(8,128)(2,1)}, bf16[1,512,256]{2,1,0:T(8,128)(2,1)}, bf16[1,512,256]{2,1,0:T(8,128)(2,1)}, f32[1,256]{1,0:T(1,128)}) custom-call(f32[1,256]{1,0:T(1,128)S(1)} %bitcast.20, f32[512,128]{1,0:T(8,128)S(1)} %get-tuple-element.27.cos_ref.refs_1_, ...), custom_call_target="tpu_custom_call", output_to_operand_aliasing={{0}: (11, {}), {1}: (12, {}), {2}: (13, {})} | custom-call | tf_op jit(solution)/shard_map/final/pallas_call | solution.py:377
  (1 shorter events, 0.0 us)
Async XLA Ops:
  3.1 0.7 %copy-start.3 = (f32[768,128]{1,0:T(8,128)}, f32[768,128]{1,0:T(8,128)S(1)}, u32[]{:S(2)}) copy-start(f32[768,128]{1,0:T(8,128)S(1)} %get-tuple-element.37) | copy-start | bytes 1179652
  3.8 20.3 %copy-start = (bf16[1,512,256]{2,1,0:T(8,128)(2,1)S(1)}, bf16[1,512,256]{2,1,0:T(8,128)(2,1)}, u32[]{:S(2)}) copy-start(bf16[1,512,256]{2,1,0:T(8,128)(2,1)} %refs_4_.3) | copy-start | bytes 786436
  3.8 20.3 %copy-start.1 = (bf16[1,512,256]{2,1,0:T(8,128)(2,1)S(1)}, bf16[1,512,256]{2,1,0:T(8,128)(2,1)}, u32[]{:S(2)}) copy-start(bf16[1,512,256]{2,1,0:T(8,128)(2,1)} %refs_5_.3) | copy-start | bytes 786436
  3.8 20.3 %copy-start.2 = (bf16[1,512,256]{2,1,0:T(8,128)(2,1)S(1)}, bf16[1,512,256]{2,1,0:T(8,128)(2,1)}, u32[]{:S(2)}) copy-start(bf16[1,512,256]{2,1,0:T(8,128)(2,1)} %q_ref.1) | copy-start | bytes 786436
  3.8 27.2 %all-to-all-start = ((f32[64,1,1536]{2,1,0:T(1,128)}), f32[64,1,1536]{2,1,0:T(1,128)S(1)}, u32[]{:S(2)}, u32[]{:S(2)}) async-start(f32[64,1,1536]{2,1,0:T(1,128)} %bitcast.13), calls=%async_computation | async-start | bytes 786432 | tf_op jit(solution)/shard_map/all_to_all | solution.py:282
  24.1 0.7 %copy-start.4 = (f32[256]{0:T(256)S(1)}, f32[256]{0:T(256)}, u32[]{:S(2)}) copy-start(f32[256]{0:T(256)} %param.12) | copy-start | bytes 3076

commit v8 on v7

--- a/solution.py
+++ b/solution.py
@@ -242,10 +242,12 @@
         copy.wait()
 
 
-def waiting_kernel(scale, *refs):
+def waiting_kernel(scale, count, *refs):
+    gain_kernel(count, refs[9], refs[13])
+
     @pl.when(local_here(False))
     def _():
-        write_grads(scale, *refs)
+        write_grads(scale, *refs[:13], *refs[14:])
 
 
 def final_kernel(scale, factor, *refs):
@@ -349,29 +351,19 @@
 
     states = exchange(scanned, "ctx", order)
 
-    gain_part = pl.pallas_call(
-        functools.partial(gain_kernel, shards),
-        out_shape=shape(groups * HEADS, DIM),
-        in_specs=[VMEM],
-        out_specs=VMEM,
-        compiler_params=PARAMS,
-        name="gain_part",
-    )(states)
-
     operands = (gain_row, cosine, sine, krot, values, out_grad, dq, dk, dv, states)
     grad_shapes = (shape(*tokens, dtype=jnp.bfloat16),) * 3
     scratch = [pltpu.VMEM(tokens, jnp.bfloat16)] * 3 + [pltpu.SemaphoreType.DMA((3 * CHUNKS,))]
-    grads = pl.pallas_call(
-        functools.partial(waiting_kernel, scale),
-        out_shape=grad_shapes,
+    *grads, gain_part = pl.pallas_call(
+        functools.partial(waiting_kernel, scale, shards),
+        out_shape=grad_shapes + (shape(groups * HEADS, DIM),),
         in_specs=[VMEM] * 10,
-        out_specs=(HBM,) * 3,
+        out_specs=(HBM,) * 3 + (VMEM,),
         scratch_shapes=scratch,
         compiler_params=PARAMS,
         name="final_core1",
     )(*operands)
 
-    gain_part, grads = lax.optimization_barrier((gain_part, grads))
     gain_parts = exchange(gain_part, "dp", [(FIRST_DP + i) % groups for i in range(groups)])
 
     grad_queries, grad_keys, grad_values, grad_gain = pl.pallas_call(

time: 60.7 us -> 60.7 us (level)
    pallas_call x2 -> x1, Pallas kernels: 1.29 us -> 1.28 us  [local(): pl.pallas_call(functools.partial(waiting_kernel, scale, shards), out_shap...]
where the time goes in v8:
time: 60.7 us; the launch traced here: 60.4 us
  blocking collectives  27.2 us (45%)
  starting transfers between devices  20.3 us (33%)
  Pallas kernels  5.7 us (9%)
  waiting for transfers between devices  4.43 us (7%)
  local copies, waits for them, and re-layouts  1.4 us (2%)
  between operations  1.36 us (2%)
    all_to_all x2, blocking collectives, exchange(): lax.all_to_all(pieces, axis, 0, 0, axis_index_groups=groups, tiled=True)  27.2 us
    all_to_all x1, starting transfers between devices, exchange(): lax.all_to_all(pieces, axis, 0, 0, axis_index_groups=groups, tiled=True)  20.3 us
    all_to_all x1, waiting for transfers between devices, exchange(): lax.all_to_all(pieces, axis, 0, 0, axis_index_groups=groups, tiled=True)  4.43 us
    pallas_call x1, Pallas kernels, local(): pl.pallas_call(functools.partial(states_kernel, scale), out_shape=(shape(...  1.8 us
    pallas_call x1, Pallas kernels, local(): pl.pallas_call(functools.partial(local_kernel, scale), out_shape=local_sh...  1.78 us
    unnamed x10, local copies, waits for them, and re-layouts  1.4 us
    pallas_call x1, Pallas kernels, local(): pl.pallas_call(functools.partial(waiting_kernel, scale, shards), out_shap...  1.28 us
  transfers between devices with their start and end apart: 1, of which 1 were waited for; matrix products, arithmetic and copies ran while one was open for 0% of the time, Pallas kernels for 3%

profile of v8, /device:TPU:1, one launch (start us, length us, event | category | flops | bytes accessed | tf_op | source)
XLA Modules:
  0.0 60.4 jit_solution(1699766949104800472)
XLA Ops:
  1.3 1.8 %states.1 = (f32[768,128]{1,0:T(8,128)S(1)}, bf16[512,256]{1,0:T(8,128)(2,1)S(1)}, f32[512,128]{1,0:T(8,128)S(1)}, f32[512,128]{1,0:T(8,128)S(1)}, f32[512,256]{...) custom-call(s32[1,1]{1,0:T(1,128)S(6)} %copy.29.off_ref, ...), custom_call_target="tpu_custom_call" | custom-call | tf_op jit(solution)/shard_map/states/pallas_call | solution.py:298
  3.1 0.0 copy-start.3
  3.1 0.7 %copy-done.3 = f32[768,128]{1,0:T(8,128)} copy-done((f32[768,128]{1,0:T(8,128)}, f32[768,128]{1,0:T(8,128)S(1)}, u32[]{:S(2)}) %copy-start.3) | copy-done | bytes 393240
  3.8 0.0 copy-start
  3.8 0.0 copy-start.1
  3.8 0.0 copy-start.2
  3.8 20.3 %all-to-all-start = ((f32[64,1,1536]{2,1,0:T(1,128)}), f32[64,1,1536]{2,1,0:T(1,128)S(1)}, u32[]{:S(2)}, u32[]{:S(2)}) async-start(f32[64,1,1536]{2,1,0:T(1,128)} %bitcast.12), calls=%async_computation | async-start | bytes 786432 | tf_op jit(solution)/shard_map/all_to_all | solution.py:284
  24.1 0.0 copy-start.4
  24.1 0.0 copy-done
  24.1 0.0 copy-done.1
  24.1 0.0 copy-done.2
  24.2 0.6 %copy-done.4 = f32[256]{0:T(256)S(1)} copy-done((f32[256]{0:T(256)S(1)}, f32[256]{0:T(256)}, u32[]{:S(2)}) %copy-start.4) | copy-done | bytes 1048
  24.8 1.8 %local_grads.1 = (f32[512,256]{1,0:T(8,128)S(1)}, f32[512,256]{1,0:T(8,128)S(1)}, f32[512,256]{1,0:T(8,128)S(1)}, f32[8,128]{1,0:T(8,128)S(1)}) custom-call(f32[1,256]{1,0:T(1,128)S(1)} %bitcast.15, f32[512,128]{1,0:T(8,128)S(1)} %get-tuple-element.24.cos_ref.refs_1_, ...), custom_call_target="tpu_custom_call", output_to_operand_aliasing={{0}: (7, {}), {1}: (8, {}), {2}: (9, {}), {3}: (10, {})} | custom-call | tf_op jit(solution)/shard_map/local_grads/pallas_call | solution.py:333
  26.6 4.4 %all-to-all-done = f32[64,1,1536]{2,1,0:T(1,128)S(1)} async-done(((f32[64,1,1536]{2,1,0:T(1,128)}), f32[64,1,1536]{2,1,0:T(1,128)S(1)}, u32[]{:S(2)}, u32[]{:S(2)}) %all-to-all-start) | async-done | bytes 393248 | tf_op jit(solution)/shard_map/all_to_all | solution.py:284
  31.0 0.2 scan.1
  31.2 17.3 %all_to_all.15 = f32[64,1,1280]{2,1,0:T(1,128)S(1)} all-to-all(f32[64,1,1280]{2,1,0:T(1,128)S(1)} %bitcast.11), channel_id=1, replica_groups={{36,37,38,39,32,33,34,35,44,45,46,47,40,41,42,43,52,53,54,55,48,49,50,5..., dimensions={0} | all-to-all | bytes 655360 | tf_op jit(solution)/shard_map/all_to_all | solution.py:284
  48.5 1.3 %final_core1.1 = (bf16[1,512,256]{2,1,0:T(8,128)(2,1)}, bf16[1,512,256]{2,1,0:T(8,128)(2,1)}, bf16[1,512,256]{2,1,0:T(8,128)(2,1)}, f32[16,128]{1,0:T(8,128)S(1)}) custom-call(f32[1,256]{1,0:T(1,128)S(1)} %bitcast.17, f32[512,128]{1,0:T(8,128)S(1)} %get-tuple-element.24.cos_ref.refs_1_, f32[512,128]{1,0:T(8,128)S(1)} %get-tuple-element.25.sin_ref.refs_2_, ...), custom_call_target="tpu_custom_call" | custom-call | tf_op jit(solution)/shard_map/final_core1/pallas_call | solution.py:357
  49.8 9.9 %all_to_all.16 = f32[8,1,256]{2,1,0:T(1,128)S(1)} all-to-all(f32[8,1,256]{2,1,0:T(1,128)S(1)} %bitcast.19), channel_id=1, replica_groups={{320,384,448,0,64,128,192,256},{321,385,449,1,65,129,193,257},{322,386,..., dimensions={0} | all-to-all | bytes 16384 | tf_op jit(solution)/shard_map/all_to_all | solution.py:284
  59.7 0.6 %final.1 = (bf16[1,512,256]{2,1,0:T(8,128)(2,1)}, bf16[1,512,256]{2,1,0:T(8,128)(2,1)}, bf16[1,512,256]{2,1,0:T(8,128)(2,1)}, f32[1,256]{1,0:T(1,128)}) custom-call(f32[1,256]{1,0:T(1,128)S(1)} %bitcast.18, f32[512,128]{1,0:T(8,128)S(1)} %get-tuple-element.24.cos_ref.refs_1_, ...), custom_call_target="tpu_custom_call", output_to_operand_aliasing={{0}: (11, {}), {1}: (12, {}), {2}: (13, {})} | custom-call | tf_op jit(solution)/shard_map/final/pallas_call | solution.py:369
Async XLA Ops:
  3.1 0.7 %copy-start.3 = (f32[768,128]{1,0:T(8,128)}, f32[768,128]{1,0:T(8,128)S(1)}, u32[]{:S(2)}) copy-start(f32[768,128]{1,0:T(8,128)S(1)} %get-tuple-element.34) | copy-start | bytes 1179652
  3.8 20.3 %copy-start = (bf16[1,512,256]{2,1,0:T(8,128)(2,1)S(1)}, bf16[1,512,256]{2,1,0:T(8,128)(2,1)}, u32[]{:S(2)}) copy-start(bf16[1,512,256]{2,1,0:T(8,128)(2,1)} %refs_4_.3) | copy-start | bytes 786436
  3.8 20.3 %copy-start.1 = (bf16[1,512,256]{2,1,0:T(8,128)(2,1)S(1)}, bf16[1,512,256]{2,1,0:T(8,128)(2,1)}, u32[]{:S(2)}) copy-start(bf16[1,512,256]{2,1,0:T(8,128)(2,1)} %refs_5_.3) | copy-start | bytes 786436
  3.8 20.3 %copy-start.2 = (bf16[1,512,256]{2,1,0:T(8,128)(2,1)S(1)}, bf16[1,512,256]{2,1,0:T(8,128)(2,1)}, u32[]{:S(2)}) copy-start(bf16[1,512,256]{2,1,0:T(8,128)(2,1)} %q_ref.1) | copy-start | bytes 786436
  3.8 27.2 %all-to-all-start = ((f32[64,1,1536]{2,1,0:T(1,128)}), f32[64,1,1536]{2,1,0:T(1,128)S(1)}, u32[]{:S(2)}, u32[]{:S(2)}) async-start(f32[64,1,1536]{2,1,0:T(1,128)} %bitcast.12), calls=%async_computation | async-start | bytes 786432 | tf_op jit(solution)/shard_map/all_to_all | solution.py:284
  24.1 0.7 %copy-start.4 = (f32[256]{0:T(256)S(1)}, f32[256]{0:T(256)}, u32[]{:S(2)}) copy-start(f32[256]{0:T(256)} %param.12) | copy-start | bytes 3076
